TPU v7x, 128 devices: a whole 4x4x4 slice. The times are simulated.
128 devices in a mesh: dp: 16 (over z, y), expert: 8 (over x, core).
Axes of the slice: x: 4, y: 4, z: 4, core: 2. Of those that a mesh axis runs over, the one named last changes fastest.
Arguments:
- tokens: bfloat16 [16384, 2048], P(('dp', 'expert')), may hold values from -6 to 6
- d_out: bfloat16 [16384, 2048], P(('dp', 'expert')), may hold values from -1.25 to 1.25
- expert_ids: int32 [16384, 8], P(('dp', 'expert')), may hold values from 0 to 127, all different within a row; in each aligned block of 128 rows (0 to 127, 128 to 255, ...) at most 9 rows name the same one
- gate_num: int32 [16384, 8], P(('dp', 'expert')), may hold values from 32 to 255
- w_gate: bfloat16 [128, 2048, 768], P(('dp', 'expert')), may hold values from -0.125 to 0.125
- w_up: bfloat16 [128, 2048, 768], P(('dp', 'expert')), may hold values from -0.125 to 0.125
- w_down: bfloat16 [128, 768, 2048], P(('dp', 'expert')), may hold values from -0.21875 to 0.21875
Outputs:
- d_tokens: bfloat16 [16384, 2048], P(('dp', 'expert'))
- d_gate: bfloat16 [16384, 8], P(('dp', 'expert'))
- d_w_gate: bfloat16 [128, 2048, 768], P(('dp', 'expert'))
- d_w_up: bfloat16 [128, 2048, 768], P(('dp', 'expert'))
- d_w_down: bfloat16 [128, 768, 2048], P(('dp', 'expert'))
Inputs may be any that keep to these rules, and one draw needn't show every extreme that they name: `expert_ids`: each row names 8 different experts; within the rows of one device no expert is named by more than 9 rows, a bound that some block reaches.
All inputs are finite; a program needn't handle non-finite values.
Results may differ from a plain program's by a relative error of at most 0.0058.
Values may be sent and summed in bfloat16 or wider, within the bound.
No kernel may reach another device: no remote copies, remote signals or barrier semaphores. Data moves between devices by JAX's collectives and lax.ppermute only.
A program may use at most 128 MiB of HBM per device.

v0:
```python
import jax
import jax.numpy as jnp
from jax import lax
from jax.sharding import PartitionSpec as P

gate_scale = 1.0 / 256.0


def expert_grads(rows_x, rows_dy, rows_gate, wg, wu, wd):
    contract_rows = (((0,), (0,)), ((), ()))
    contract_cols = (((1,), (1,)), ((), ()))
    pre_gate = jnp.dot(rows_x, wg, preferred_element_type=jnp.float32)
    pre_up = jnp.dot(rows_x, wu, preferred_element_type=jnp.float32)
    sig = jax.nn.sigmoid(pre_gate)
    active = pre_gate * sig
    hidden = active * pre_up
    back = lax.dot_general(rows_dy, wd, contract_cols, preferred_element_type=jnp.float32)
    gate_grad = jnp.sum(back * hidden, axis=1).astype(jnp.bfloat16)
    scaled = rows_gate[:, None] * back
    weighted = (rows_gate[:, None] * hidden).astype(jnp.bfloat16)
    grad_a = (scaled * pre_up * sig * (1.0 + pre_gate * (1.0 - sig))).astype(jnp.bfloat16)
    grad_b = (scaled * active).astype(jnp.bfloat16)
    grad_down = lax.dot_general(
        weighted, rows_dy, contract_rows, preferred_element_type=jnp.float32
    ).astype(jnp.bfloat16)
    grad_gate = lax.dot_general(
        rows_x, grad_a, contract_rows, preferred_element_type=jnp.float32
    ).astype(jnp.bfloat16)
    grad_up = lax.dot_general(
        rows_x, grad_b, contract_rows, preferred_element_type=jnp.float32
    ).astype(jnp.bfloat16)
    row_grad = lax.dot_general(grad_a, wg, contract_cols, preferred_element_type=jnp.float32)
    row_grad = (
        row_grad + lax.dot_general(grad_b, wu, contract_cols, preferred_element_type=jnp.float32)
    ).astype(jnp.bfloat16)
    return (row_grad, gate_grad, grad_gate, grad_up, grad_down)


def local(tokens, d_out, expert_ids, gate_num, w_gate, w_up, w_down):
    tok_rows, width = tokens.shape
    top = expert_ids.shape[1]
    dp_count = lax.axis_size("dp")
    ex_count = lax.axis_size("expert")
    experts = dp_count * ex_count
    capacity = max(2, (tok_rows * top * 9 + 8 * experts - 1) // (8 * experts))
    routes = tok_rows * top
    flat_ids = expert_ids.reshape(-1)
    onehot = (flat_ids[:, None] == jnp.arange(experts, dtype=jnp.int32)[None, :]).astype(jnp.int32)
    position = jnp.sum(jnp.cumsum(onehot, axis=0) * onehot, axis=1) - 1
    slot = flat_ids * capacity + position
    owner = (
        jnp.full((experts * capacity,), -1, jnp.int32)
        .at[slot]
        .set(jnp.arange(routes, dtype=jnp.int32))
    )
    valid = owner >= 0
    safe = jnp.where(valid, owner, 0)
    row = safe // top
    send_x = jnp.where(valid[:, None], tokens[row], jnp.zeros((), tokens.dtype))
    send_dy = jnp.where(valid[:, None], d_out[row], jnp.zeros((), d_out.dtype))
    gate_flat = gate_num.reshape(-1).astype(jnp.float32) * gate_scale
    send_gate = jnp.where(valid, gate_flat[safe], 0.0).astype(jnp.bfloat16)
    recv_x, recv_dy, recv_gate = (
        lax.all_to_all(
            send_x.reshape(experts, capacity, width),
            ("dp", "expert"),
            split_axis=0,
            concat_axis=0,
            tiled=True,
        ),
        lax.all_to_all(
            send_dy.reshape(experts, capacity, width),
            ("dp", "expert"),
            split_axis=0,
            concat_axis=0,
            tiled=True,
        ),
        lax.all_to_all(
            send_gate.reshape(experts, capacity),
            ("dp", "expert"),
            split_axis=0,
            concat_axis=0,
            tiled=True,
        ),
    )
    rows_x = recv_x.reshape(experts * capacity, width)
    rows_dy = recv_dy.reshape(experts * capacity, width)
    rows_gate = recv_gate.reshape(experts * capacity).astype(jnp.float32)
    row_grad, gate_grad, grad_gate, grad_up, grad_down = expert_grads(
        rows_x, rows_dy, rows_gate, w_gate[0], w_up[0], w_down[0]
    )
    back_rows, back_gate = (
        lax.all_to_all(
            row_grad.reshape(experts, capacity, width),
            ("dp", "expert"),
            split_axis=0,
            concat_axis=0,
            tiled=True,
        ),
        lax.all_to_all(
            gate_grad.reshape(experts, capacity),
            ("dp", "expert"),
            split_axis=0,
            concat_axis=0,
            tiled=True,
        ),
    )
    back_rows = back_rows.reshape(experts * capacity, width)
    back_gate = back_gate.reshape(experts * capacity)
    per_route = back_rows[slot].reshape(tok_rows, top, width).astype(jnp.float32)
    d_tokens = jnp.sum(per_route, axis=1).astype(jnp.bfloat16)
    d_gate = back_gate[slot].reshape(tok_rows, top)
    return (d_tokens, d_gate, grad_gate[None], grad_up[None], grad_down[None])


def solution(mesh):
    return jax.shard_map(
        local,
        mesh=mesh,
        in_specs=(
            P(("dp", "expert"), None),
            P(("dp", "expert"), None),
            P(("dp", "expert"), None),
            P(("dp", "expert"), None),
            P(("dp", "expert"), None, None),
            P(("dp", "expert"), None, None),
            P(("dp", "expert"), None, None),
        ),
        out_specs=(
            P(("dp", "expert"), None),
            P(("dp", "expert"), None),
            P(("dp", "expert"), None, None),
            P(("dp", "expert"), None, None),
            P(("dp", "expert"), None, None),
        ),
        check_vma=False,
    )
```

profile of v0, /device:TPU:90, one launch (start us, length us, event | category | flops | bytes accessed | tf_op | source)
XLA Modules:
  0.0 486.3 jit_solution(12857236386768668115)
XLA Ops:
  1.5 0.9 copy.20
  4.8 1.1 broadcast_add_fusion
  6.4 4.3 scatter_custom_fusion
  10.8 7.3 %gather_fusion = bf16[1152]{0:T(1024)(128)(2,1)S(1)} fusion(bf16[1024]{0:T(1024)(128)(2,1)S(1)} %mul.72, s32[2048]{0:T(1024)S(1)} %pad_clamp_fusion.1), kind=kCustom, calls=%fused_computation | custom fusion | bytes 9216 | tf_op jit(solution)/shard_map/gather | solution.py:62
  19.0 9.9 %all-to-all-start = ((bf16[128,1,9]{2,1,0:T(2,128)(2,1)}), bf16[128,1,9]{2,1,0:T(2,128)(2,1)S(1)}, u32[]{:S(2)}, u32[]{:S(2)}) async-start(bf16[128,1,9]{2,1,0:T(2,128)(2,1)} %all_to_all.25), calls=%async_computation | async-start | bytes 131072 | tf_op jit(solution)/shard_map/all_to_all | solution.py:78
  29.1 11.8 %gather_fusion.2 = bf16[1152,2048]{1,0:T(8,128)(2,1)} fusion(bf16[128,2048]{1,0:T(8,128)(2,1)} %param.7, s32[2048]{0:T(1024)S(1)} %pad_clamp_fusion), kind=kCustom, calls=%fused_computation.2 | custom fusion | bytes 9441792 | tf_op jit(solution)/shard_map/gather | solution.py:59
  40.9 8.1 %gather.23 = bf16[128,9,2048]{2,1,0:T(8,128)(2,1)} reshape(bf16[1152,2048]{1,0:T(8,128)(2,1)} %gather_fusion.2) | data formatting | bytes 9437184 | tf_op jit(solution)/shard_map/gather | solution.py:59
  49.0 11.8 %gather_fusion.1 = bf16[1152,2048]{1,0:T(8,128)(2,1)} fusion(bf16[128,2048]{1,0:T(8,128)(2,1)} %param.8, s32[2048]{0:T(1024)S(1)} %pad_clamp_fusion), kind=kCustom, calls=%fused_computation.1 | custom fusion | bytes 9441792 | tf_op jit(solution)/shard_map/gather | solution.py:60
  60.8 8.1 %gather.21 = bf16[128,9,2048]{2,1,0:T(8,128)(2,1)} reshape(bf16[1152,2048]{1,0:T(8,128)(2,1)} %gather_fusion.1) | data formatting | bytes 9437184 | tf_op jit(solution)/shard_map/gather | solution.py:60
  68.8 11.4 %broadcast_select_fusion.1 = (bf16[128,9,2048]{2,1,0:T(8,128)(2,1)}, bf16[128,9,2048]{2,1,0:T(8,128)(2,1)}) fusion(bf16[128,9,2048]{2,1,0:T(8,128)(2,1)} %gather.21, pred[128,9]{1,0:T(8,128)(4,1)S(1)} %broadcast_in_dim.54, bf16[128,9,2048]{2,1,0:T(8,128)(2,1)} %gather.23), kind=kLoop, calls=%fused_computation.8 | loop fusion | flops 4718592 | bytes 18875520 | tf_op jit(solution)/shard_map/jit(_where)/select_n | solution.py:60
  80.3 102.6 %all_to_all.31 = bf16[128,9,2048]{2,1,0:T(8,128)(2,1)} all-to-all(bf16[128,9,2048]{2,1,0:T(8,128)(2,1)} %get-tuple-element.21), channel_id=1, replica_groups=mesh['dp'=16,'expert'=8] {'dp','expert'}, dimensions={0} | all-to-all | bytes 9437184 | tf_op jit(solution)/shard_map/all_to_all | solution.py:64
  182.9 11.3 %all-to-all-start.1 = ((bf16[128,9,2048]{2,1,0:T(8,128)(2,1)}), bf16[128,9,2048]{2,1,0:T(8,128)(2,1)}, u32[]{:S(2)}, u32[]{:S(2)}) async-start(bf16[128,9,2048]{2,1,0:T(8,128)(2,1)} %get-tuple-element.20), calls=%async_computation.1 | async-start | bytes 16777216 | tf_op jit(solution)/shard_map/all_to_all | solution.py:71
  194.6 8.4 %reshape.131 = bf16[1152,2048]{1,0:T(8,128)(2,1)} reshape(bf16[128,9,2048]{2,1,0:T(8,128)(2,1)} %all_to_all.31) | data formatting | bytes 9437184 | tf_op jit(solution)/shard_map/reshape | solution.py:86
  203.0 8.5 %fusion.3 = f32[1152,768]{0,1:T(8,128)} fusion(bf16[1152,2048]{1,0:T(8,128)(2,1)} %reshape.131, bf16[1,2048,768]{2,1,0:T(8,128)(2,1)S(1)} %copy-done), kind=kOutput, calls=%fused_computation.21 | convolution fusion | flops 3623878656 | bytes 11403264 | tf_op jit(solution)/shard_map/dot_general | solution.py:12
  211.5 6.3 %fusion.6 = f32[1152,768]{0,1:T(8,128)} fusion(bf16[1152,2048]{1,0:T(8,128)(2,1)S(1)} %copy-done.2, bf16[1,2048,768]{2,1,0:T(8,128)(2,1)S(1)} %copy-done.4), kind=kOutput, calls=%fused_computation.24 | convolution fusion | flops 3623878656 | bytes 11403264 | tf_op jit(solution)/shard_map/dot_general | solution.py:13
  217.9 78.7 %all-to-all-done.1 = bf16[128,9,2048]{2,1,0:T(8,128)(2,1)} async-done(((bf16[128,9,2048]{2,1,0:T(8,128)(2,1)}), bf16[128,9,2048]{2,1,0:T(8,128)(2,1)}, u32[]{:S(2)}, u32[]{:S(2)}) %all-to-all-start.1) | async-done | bytes 4718624 | tf_op jit(solution)/shard_map/all_to_all | solution.py:71
  296.5 8.7 %reshape.130 = bf16[1152,2048]{1,0:T(8,128)(2,1)} reshape(bf16[128,9,2048]{2,1,0:T(8,128)(2,1)} %all-to-all-done.1) | data formatting | bytes 9437184 | tf_op jit(solution)/shard_map/reshape | solution.py:87
  305.2 12.6 %multiply_reduce_fusion = (bf16[1152]{0:T(1024)(128)(2,1)S(1)}, bf16[1152,768]{0,1:T(8,128)(2,1)}, bf16[1152,768]{0,1:T(8,128)(2,1)}) fusion(f32[1152,768]{0,1:T(8,128)} %fusion.6, f32[1152,768]{0,1:T(8,128)} %fusion.3, f32[1152]{0:T(1024)S(1)} %reshape.137, bf16[1152,2048]{1,0:T(8,128)(2,1)} %reshape.130, bf16[1,768,2048]{2,1,0:T(8,128)(2,1)} %param.13), kind=kOutput, calls=%fused_computation.11 | convolution fusion | flops 3638918144 | bytes 18488064 | tf_op jit(solution)/shard_map/dot_general | solution.py:17
  317.8 0.9 convert_element_type.74
  318.7 8.4 %all-to-all-start.4 = ((bf16[128,1,9]{2,1,0:T(2,128)(2,1)}), bf16[128,1,9]{2,1,0:T(2,128)(2,1)S(1)}, u32[]{:S(2)}, u32[]{:S(2)}) async-start(bf16[128,1,9]{2,1,0:T(2,128)(2,1)} %convert_element_type.74), calls=%async_computation.4 | async-start | bytes 131072 | tf_op jit(solution)/shard_map/all_to_all | solution.py:100
  327.2 5.6 %fusion.1 = f32[1152,2048]{1,0:T(8,128)S(1)} fusion(bf16[1152,768]{0,1:T(8,128)(2,1)} %get-tuple-element.18, bf16[1,2048,768]{2,1,0:T(8,128)(2,1)S(1)} %copy-done), kind=kOutput, calls=%fused_computation.19 | convolution fusion | flops 3623878656 | bytes 14352384 | tf_op jit(solution)/shard_map/dot_general | solution.py:32
  332.8 5.7 %add_convert_fusion = bf16[1152,2048]{1,0:T(8,128)(2,1)} fusion(f32[1152,2048]{1,0:T(8,128)S(1)} %fusion.1, bf16[1152,768]{0,1:T(8,128)(2,1)S(1)} %copy-done.9, bf16[1,2048,768]{2,1,0:T(8,128)(2,1)S(1)} %copy-done.5), kind=kOutput, calls=%fused_computation.6 | convolution fusion | flops 3628597248 | bytes 19070976 | tf_op jit(solution)/shard_map/dot_general | solution.py:34
  338.5 8.1 %reshape.132 = bf16[128,9,2048]{2,1,0:T(8,128)(2,1)} reshape(bf16[1152,2048]{1,0:T(8,128)(2,1)} %add_convert_fusion) | data formatting | bytes 9437184 | tf_op jit(solution)/shard_map/reshape | solution.py:94
  346.6 10.7 %all-to-all-start.3 = ((bf16[128,9,2048]{2,1,0:T(8,128)(2,1)}), bf16[128,9,2048]{2,1,0:T(8,128)(2,1)}, u32[]{:S(2)}, u32[]{:S(2)}) async-start(bf16[128,9,2048]{2,1,0:T(8,128)(2,1)} %reshape.132), calls=%async_computation.3 | async-start | bytes 16777216 | tf_op jit(solution)/shard_map/all_to_all | solution.py:93
  357.3 8.3 %fusion.10 = bf16[1,2048,768]{2,1,0:T(8,128)(2,1)} fusion(bf16[1152,2048]{1,0:T(8,128)(2,1)} %reshape.131, bf16[1152,768]{0,1:T(8,128)(2,1)S(1)} %copy-done.6), kind=kOutput, calls=%fused_computation.28 | convolution fusion | flops 3625451520 | bytes 9633792 | tf_op jit(solution)/shard_map/dot_general | solution.py:26
  365.6 8.3 %fusion.11 = bf16[1,2048,768]{2,1,0:T(8,128)(2,1)} fusion(bf16[1152,2048]{1,0:T(8,128)(2,1)} %reshape.131, bf16[1152,768]{0,1:T(8,128)(2,1)S(1)} %copy-done.10), kind=kOutput, calls=%fused_computation.29 | convolution fusion | flops 3625451520 | bytes 9633792 | tf_op jit(solution)/shard_map/dot_general | solution.py:29
  373.9 5.8 %fusion.12 = bf16[1,768,2048]{2,1,0:T(8,128)(2,1)} fusion(bf16[1152,2048]{1,0:T(8,128)(2,1)S(1)} %bitcast.45, f32[1152]{0:T(1024)S(1)} %reshape.137, f32[1152,768]{0,1:T(8,128)S(1)} %copy-done.8, f32[1152,768]{0,1:T(8,128)S(1)} %copy-done.7), kind=kOutput, calls=%fused_computation.30 | convolution fusion | flops 3631644672 | bytes 14946816 | tf_op jit(solution)/shard_map/dot_general | solution.py:23
  380.1 6.8 %gather_fusion.4 = bf16[1024]{0:T(1024)(128)(2,1)S(1)} fusion(bf16[1152]{0:T(1024)(128)(2,1)S(1)} %reshape.135, s32[1024]{0:T(1024)S(1)} %broadcast_clamp_fusion), kind=kCustom, calls=%fused_computation.4 | custom fusion | bytes 8192 | tf_op jit(solution)/shard_map/gather | solution.py:112
  387.7 71.9 %all-to-all-done.3 = bf16[128,9,2048]{2,1,0:T(8,128)(2,1)} async-done(((bf16[128,9,2048]{2,1,0:T(8,128)(2,1)}), bf16[128,9,2048]{2,1,0:T(8,128)(2,1)}, u32[]{:S(2)}, u32[]{:S(2)}) %all-to-all-start.3) | async-done | bytes 4718624 | tf_op jit(solution)/shard_map/all_to_all | solution.py:93
  459.6 8.4 %reshape.133 = bf16[1152,2048]{1,0:T(8,128)(2,1)} reshape(bf16[128,9,2048]{2,1,0:T(8,128)(2,1)} %all-to-all-done.3) | data formatting | bytes 9437184 | tf_op jit(solution)/shard_map/reshape | solution.py:108
  468.0 11.9 %gather_fusion.3 = bf16[1024,2048]{1,0:T(8,128)(2,1)} fusion(bf16[1152,2048]{1,0:T(8,128)(2,1)} %reshape.133, s32[1024]{0:T(1024)S(1)} %broadcast_clamp_fusion), kind=kCustom, calls=%fused_computation.3 | custom fusion | bytes 8392704 | tf_op jit(solution)/shard_map/gather | solution.py:110
  479.9 5.9 %bitcast_reduce_fusion = bf16[128,2048]{1,0:T(8,128)(2,1)} fusion(bf16[1024,2048]{1,0:T(8,128)(2,1)} %gather_fusion.3), kind=kLoop, calls=%fused_computation.9 | loop fusion | flops 1835008 | bytes 4718592 | tf_op jit(solution)/shard_map/reduce_sum | solution.py:111
  (61 shorter events, 6.5 us)
Async XLA Ops:
  0.6 202.3 %copy-start = (bf16[1,2048,768]{2,1,0:T(8,128)(2,1)S(1)}, bf16[1,2048,768]{2,1,0:T(8,128)(2,1)}, u32[]{:S(2)}) copy-start(bf16[1,2048,768]{2,1,0:T(8,128)(2,1)} %param.11) | copy-start | bytes 9437188
  4.0 0.8 copy-start.3
  19.0 61.3 %all-to-all-start = ((bf16[128,1,9]{2,1,0:T(2,128)(2,1)}), bf16[128,1,9]{2,1,0:T(2,128)(2,1)S(1)}, u32[]{:S(2)}, u32[]{:S(2)}) async-start(bf16[128,1,9]{2,1,0:T(2,128)(2,1)} %all_to_all.25), calls=%async_computation | async-start | bytes 131072 | tf_op jit(solution)/shard_map/all_to_all | solution.py:78
  182.9 113.6 %all-to-all-start.1 = ((bf16[128,9,2048]{2,1,0:T(8,128)(2,1)}), bf16[128,9,2048]{2,1,0:T(8,128)(2,1)}, u32[]{:S(2)}, u32[]{:S(2)}) async-start(bf16[128,9,2048]{2,1,0:T(8,128)(2,1)} %get-tuple-element.20), calls=%async_computation.1 | async-start | bytes 16777216 | tf_op jit(solution)/shard_map/all_to_all | solution.py:71
  203.0 8.5 %copy-start.2 = (bf16[1152,2048]{1,0:T(8,128)(2,1)S(1)}, bf16[1152,2048]{1,0:T(8,128)(2,1)}, u32[]{:S(2)}) copy-start(bf16[1152,2048]{1,0:T(8,128)(2,1)} %reshape.131) | copy-start | bytes 14155780
  203.0 8.5 %copy-start.4 = (bf16[1,2048,768]{2,1,0:T(8,128)(2,1)S(1)}, bf16[1,2048,768]{2,1,0:T(8,128)(2,1)}, u32[]{:S(2)}) copy-start(bf16[1,2048,768]{2,1,0:T(8,128)(2,1)} %param.12) | copy-start | bytes 9437188
  318.7 27.9 %all-to-all-start.4 = ((bf16[128,1,9]{2,1,0:T(2,128)(2,1)}), bf16[128,1,9]{2,1,0:T(2,128)(2,1)S(1)}, u32[]{:S(2)}, u32[]{:S(2)}) async-start(bf16[128,1,9]{2,1,0:T(2,128)(2,1)} %convert_element_type.74), calls=%async_computation.4 | async-start | bytes 131072 | tf_op jit(solution)/shard_map/all_to_all | solution.py:100
  327.1 5.6 %copy-start.5 = (bf16[1,2048,768]{2,1,0:T(8,128)(2,1)S(1)}, bf16[1,2048,768]{2,1,0:T(8,128)(2,1)}, u32[]{:S(2)}) copy-start(bf16[1,2048,768]{2,1,0:T(8,128)(2,1)} %param.12) | copy-start | bytes 9437188
  327.2 5.6 %copy-start.9 = (bf16[1152,768]{0,1:T(8,128)(2,1)S(1)}, bf16[1152,768]{0,1:T(8,128)(2,1)}, u32[]{:S(2)}) copy-start(bf16[1152,768]{0,1:T(8,128)(2,1)} %get-tuple-element.19) | copy-start | bytes 5308420
  346.6 10.7 %copy-start.6 = (bf16[1152,768]{0,1:T(8,128)(2,1)S(1)}, bf16[1152,768]{0,1:T(8,128)(2,1)}, u32[]{:S(2)}) copy-start(bf16[1152,768]{0,1:T(8,128)(2,1)} %get-tuple-element.18) | copy-start | bytes 5308420
  346.6 113.0 %all-to-all-start.3 = ((bf16[128,9,2048]{2,1,0:T(8,128)(2,1)}), bf16[128,9,2048]{2,1,0:T(8,128)(2,1)}, u32[]{:S(2)}, u32[]{:S(2)}) async-start(bf16[128,9,2048]{2,1,0:T(8,128)(2,1)} %reshape.132), calls=%async_computation.3 | async-start | bytes 16777216 | tf_op jit(solution)/shard_map/all_to_all | solution.py:93
  357.3 8.3 %copy-start.10 = (bf16[1152,768]{0,1:T(8,128)(2,1)S(1)}, bf16[1152,768]{0,1:T(8,128)(2,1)}, u32[]{:S(2)}) copy-start(bf16[1152,768]{0,1:T(8,128)(2,1)} %get-tuple-element.19) | copy-start | bytes 5308420
  357.3 16.6 %slice-start = ((s8[4718592]{0:T(1024)(128)(4,1)}), s8[4194304]{0:T(1024)(128)(4,1)S(1)}, s32[]{:S(2)}) async-start(s8[4718592]{0:T(1024)(128)(4,1)} %bitcast.44), calls=%async_computation.5 | async-start | bytes 8388608
  365.6 8.3 %slice-start.1 = ((s8[4718592]{0:T(1024)(128)(4,1)}), s8[524288]{0:T(1024)(128)(4,1)S(1)}, s32[]{:S(2)}) async-start(s8[4718592]{0:T(1024)(128)(4,1)} %bitcast.44), calls=%async_computation.6 | async-start | bytes 1048576
  365.6 8.3 %copy-start.7 = (f32[1152,768]{0,1:T(8,128)S(1)}, f32[1152,768]{0,1:T(8,128)}, u32[]{:S(2)}) copy-start(f32[1152,768]{0,1:T(8,128)} %fusion.3) | copy-start | bytes 10616836
  365.6 8.3 %copy-start.8 = (f32[1152,768]{0,1:T(8,128)S(1)}, f32[1152,768]{0,1:T(8,128)}, u32[]{:S(2)}) copy-start(f32[1152,768]{0,1:T(8,128)} %fusion.6) | copy-start | bytes 10616836
  468.0 17.8 %copy-start.1 = (bf16[1,2048,768]{2,1,0:T(8,128)(2,1)S(1)}, bf16[1,2048,768]{2,1,0:T(8,128)(2,1)}, u32[]{:S(2)}) copy-start(bf16[1,2048,768]{2,1,0:T(8,128)(2,1)} %param.11) | copy-start | bytes 9437188
where the time goes:
time: 495 us; the launch traced here: 486 us
  waiting for transfers between devices  151 us (31%)
  local copies, waits for them, and re-layouts  109 us (22%)
  blocking collectives  103 us (21%)
  matrix products  61.1 us (12%)
  starting transfers between devices  40.3 us (8%)
  other arithmetic  21 us (4%)
    all_to_all x1, blocking collectives, local(): lax.all_to_all(send_x.reshape(experts, capacity, width), ('dp', 'expert')...  103 us
    all_to_all x1, waiting for transfers between devices, local(): lax.all_to_all(send_dy.reshape(experts, capacity, width), ('dp', 'expert'...  78.7 us
    all_to_all x1, waiting for transfers between devices, local(): lax.all_to_all(row_grad.reshape(experts, capacity, width), ('dp', 'expert...  71.9 us
    gather x2, local copies, waits for them, and re-layouts, local(): send_x = jnp.where(valid[:, None], tokens[row], jnp.zeros((), tokens.dtype))  19.9 us
    gather x2, local copies, waits for them, and re-layouts, local(): send_dy = jnp.where(valid[:, None], d_out[row], jnp.zeros((), d_out.dtype))  19.8 us
    dot_general x1, matrix products, expert_grads(): lax.dot_general(rows_dy, wd, contract_cols, preferred_element_type=jnp.fl...  12.6 us
    gather x1, local copies, waits for them, and re-layouts, local(): back_rows[slot].reshape(tok_rows, top, width).astype(jnp.float32)  11.9 us
    select_n x2, other arithmetic, local(): send_dy = jnp.where(valid[:, None], d_out[row], jnp.zeros((), d_out.dtype))  11.5 us
  transfers between devices with their start and end apart: 4, of which 2 were waited for; matrix products, arithmetic and copies ran while one was open for 26% of the time, Pallas kernels for 0%

commit v1 on v0

v1 whole, which is shorter than its diff:
```python
import functools

import jax
import jax.numpy as jnp
from jax import lax
from jax.experimental import pallas as pl
from jax.experimental.pallas import tpu as pltpu
from jax.sharding import PartitionSpec as P

bf16 = jnp.bfloat16
f32 = jnp.float32
lanes = 128
sub = 16
capacity = 9
first_rows = 7
contract_rows = (((0,), (0,)), ((), ()))
contract_cols = (((1,), (1,)), ((), ()))


def params(mib):
    return pltpu.CompilerParams(vmem_limit_bytes=mib * 1024 * 1024)


def whole(shape):
    return pl.BlockSpec(shape, lambda *_: (0,) * len(shape))


def swap_matrix():
    size = sub * sub
    row = lax.broadcasted_iota(jnp.int32, (size, size), 0)
    col = lax.broadcasted_iota(jnp.int32, (size, size), 1)
    return jnp.where(((row & 15) << 4) + (row >> 4) == col, 1.0, 0.0).astype(bf16)


def spread_tables(ids, num, experts):
    top, toks = ids.shape
    gate = num.astype(f32) * (1.0 / 256.0)
    expert_at = lax.broadcasted_iota(jnp.int32, (experts, toks), 0)
    named = jnp.zeros((experts, toks), f32)
    gates = jnp.zeros((experts, toks), f32)
    for k in range(top):
        hit = ids[k : k + 1, :] == expert_at
        named = jnp.where(hit, 1.0, named)
        gates = jnp.where(hit, gate[k : k + 1, :], gates)
    row = lax.broadcasted_iota(jnp.int32, (toks, toks), 0)
    col = lax.broadcasted_iota(jnp.int32, (toks, toks), 1)
    before = jnp.where(row < col, 1.0, 0.0).astype(bf16)
    place = jnp.dot(named.astype(bf16), before, preferred_element_type=f32)
    token = lax.broadcasted_iota(jnp.int32, (experts, toks), 1).astype(f32)
    here = [(named > 0.0) & (place == float(p)) for p in range(capacity)]
    wanted = lax.broadcasted_iota(jnp.int32, (sub, capacity * toks), 0)
    owner = lax.broadcasted_iota(jnp.int32, (sub, capacity * toks), 1) >> 7
    collect = jnp.where(owner == wanted, 1.0, 0.0).astype(bf16)
    index, scale = [
        lax.dot_general(
            collect,
            jnp.concatenate([jnp.where(h, v, 0.0).astype(bf16) for h in here], axis=1),
            contract_cols,
            preferred_element_type=f32,
        )
        for v in (token, gates)
    ]
    code = (expert_at * sub).astype(f32) + place
    codes = [
        jnp.sum(jnp.where(ids[k : k + 1, :] == expert_at, code, 0.0), axis=0, keepdims=True)
        for k in range(top)
    ]
    return index.astype(jnp.int32), scale, jnp.concatenate(codes, axis=0).astype(jnp.int32)


def wide_to_tiles(swap, wide, chunks, store):
    rows = wide.shape[0]
    for r in range(0, rows, 2 * sub):
        halves = [
            jnp.concatenate(
                [wide[r + d : r + d + sub, j * lanes : (j + 1) * lanes] for j in range(chunks)], axis=0
            )
            for d in (0, sub)
        ]
        tiles = jnp.dot(swap, jnp.concatenate(halves, axis=1), preferred_element_type=f32)
        store(r, tiles[:, :lanes].reshape(sub, chunks, lanes))
        store(r + sub, tiles[:, lanes:].reshape(sub, chunks, lanes))


def make_tiles(tok_ref, dy_ref, tok_tiles, dy_tiles):
    swap = swap_matrix()
    chunks = tok_ref.shape[1] // lanes

    def put_tok(r, tiles):
        tok_tiles[r : r + sub] = tiles.astype(bf16)

    def put_dy(r, tiles):
        dy_tiles[r : r + sub] = tiles

    wide_to_tiles(swap, tok_ref, chunks, put_tok)
    wide_to_tiles(swap, dy_ref, chunks, put_dy)


def fill_rows(start, count, index_ref, scale_ref, tok_tiles, dy_tiles, out_ref):
    group = out_ref.shape[0]
    first = pl.program_id(0) * group

    def one(e, carry):
        for p in range(count):
            token = index_ref[start + p, first + e]
            scale = scale_ref[start + p, first + e]
            out_ref[e, p * sub : (p + 1) * sub, :] = tok_tiles[token]
            at = (count + p) * sub
            out_ref[e, at : at + sub, :] = (dy_tiles[token] * scale).astype(bf16)
        return carry

    lax.fori_loop(0, group, one, 0)


def pack_first_kernel(
    start, count, ids_ref, num_ref, tok_ref, dy_ref,
    out_ref, index_ref, scale_ref, code_ref, tok_tiles, dy_tiles, index_s, scale_s, sems,
):
    @pl.when(pl.program_id(0) == 0)
    def _():
        index, scale, code = spread_tables(ids_ref[...], num_ref[...], index_ref.shape[1])
        index_ref[...] = index
        scale_ref[...] = scale
        code_ref[...] = code
        one = pltpu.make_async_copy(index_ref, index_s, sems.at[0])
        two = pltpu.make_async_copy(scale_ref, scale_s, sems.at[1])
        one.start()
        two.start()
        make_tiles(tok_ref, dy_ref, tok_tiles, dy_tiles)
        one.wait()
        two.wait()

    fill_rows(start, count, index_s, scale_s, tok_tiles, dy_tiles, out_ref)


def pack_rest_kernel(
    start, count, index_ref, scale_ref, tok_ref, dy_ref, out_ref, tok_tiles, dy_tiles
):
    @pl.when(pl.program_id(0) == 0)
    def _():
        make_tiles(tok_ref, dy_ref, tok_tiles, dy_tiles)

    fill_rows(start, count, index_ref, scale_ref, tok_tiles, dy_tiles, out_ref)


def pack(tokens, d_out, start, count, experts, ids=None, num=None, tables=None):
    toks, width = tokens.shape
    chunks = width // lanes
    group = 16
    out_shape = [jax.ShapeDtypeStruct((experts, 2 * count * sub, lanes), bf16)]
    out_specs = [pl.BlockSpec((group, 2 * count * sub, lanes), lambda i: (i, 0, 0))]
    scratch = [
        pltpu.VMEM((toks, chunks, lanes), bf16),
        pltpu.VMEM((toks, chunks, lanes), f32),
    ]
    if tables is None:
        body = functools.partial(pack_first_kernel, start, count)
        args = (ids, num, tokens, d_out)
        in_specs = [whole(a.shape) for a in args]
        out_shape += [
            jax.ShapeDtypeStruct((sub, experts), jnp.int32),
            jax.ShapeDtypeStruct((sub, experts), f32),
            jax.ShapeDtypeStruct(ids.shape, jnp.int32),
        ]
        out_specs += [whole(o.shape) for o in out_shape[1:]]
        scratch += [
            pltpu.SMEM((sub, experts), jnp.int32),
            pltpu.SMEM((sub, experts), f32),
            pltpu.SemaphoreType.DMA((2,)),
        ]
    else:
        body = functools.partial(pack_rest_kernel, start, count)
        args = (*tables, tokens, d_out)
        in_specs = [pl.BlockSpec(memory_space=pltpu.SMEM)] * 2 + [whole(tokens.shape)] * 2
    return pl.pallas_call(
        body,
        grid=(experts // group,),
        in_specs=in_specs,
        out_specs=out_specs,
        out_shape=out_shape,
        scratch_shapes=scratch,
        compiler_params=params(60),
        cost_estimate=pl.CostEstimate(
            flops=0, bytes_accessed=4 * experts * count * width, transcendentals=0
        ),
        name="pack_first" if tables is None else "pack_rest",
    )(*args)


def expert_kernel(start, count, block, last, *refs):
    (wire_hbm, wg_hbm, wu_hbm, wd_hbm) = refs[:4]
    refs = refs[4:]
    if last:
        old_gate_ref = refs[0]
        refs = refs[7:]
    out_hbm = refs[:5]
    back_ref = refs[5]
    refs = refs[6:]
    if not last:
        gate_ref = refs[0]
        refs = refs[1:]
    (wire, wg, wu, wd, x_ref, dy_ref, h_ref, da_ref, db_ref, dx_ref, swap_ref) = refs[:11]
    (wire_sem, weight_sem, out_sem) = refs[11:]
    sources = wire_hbm.shape[0]
    blocks = sources // block
    rows = block * count
    width, hidden = wg.shape
    chunks = width // lanes
    part = 256
    half = count * sub

    def wire_copy(b, side):
        at = (slice(b * block, (b + 1) * block), slice(side * half, (side + 1) * half))
        return pltpu.make_async_copy(wire_hbm.at[at], wire.at[at], wire_sem.at[b, side])

    weights = [
        pltpu.make_async_copy(src, dst, weight_sem.at[i])
        for i, (src, dst) in enumerate(((wg_hbm, wg), (wu_hbm, wu), (wd_hbm, wd)))
    ]

    def out_copy(i, b):
        src = (x_ref, dy_ref, h_ref, da_ref, db_ref)[i]
        to = sources * start + b * rows
        return pltpu.make_async_copy(
            src.at[b * rows : (b + 1) * rows], out_hbm[i].at[to : to + rows], out_sem.at[i, b]
        )

    wire_copy(0, 0).start()
    weights[0].start()
    weights[1].start()
    wire_copy(0, 1).start()
    weights[2].start()
    for b in range(1, blocks):
        wire_copy(b, 0).start()
        wire_copy(b, 1).start()
    swap_ref[...] = swap_matrix()

    def widen(b, side, out):
        def step(p, carry):
            at = pl.multiple_of(side * half + p * sub, sub)
            for s in range(0, block, 2 * sub):
                tiles = jnp.concatenate(
                    [
                        wire[b * block + s + d : b * block + s + d + sub, pl.ds(at, sub), :].reshape(
                            sub * sub, lanes
                        )
                        for d in (0, sub)
                    ],
                    axis=1,
                )
                flat = jnp.dot(swap_ref[...], tiles, preferred_element_type=f32).astype(bf16)
                for d in (0, 1):
                    to = pl.multiple_of(b * rows + p * block + s + d * sub, sub)
                    for j in range(chunks):
                        out[pl.ds(to, sub), j * lanes : (j + 1) * lanes] = flat[
                            j * sub : (j + 1) * sub, d * lanes : (d + 1) * lanes
                        ]
            return carry

        lax.fori_loop(0, count, step, 0)

    for b in range(blocks):
        low, high = b * rows, (b + 1) * rows
        wire_copy(b, 0).wait()
        widen(b, 0, x_ref)
        out_copy(0, b).start()
        wire_copy(b, 1).wait()
        widen(b, 1, dy_ref)
        out_copy(1, b).start()
        if b == 0:
            for copy in weights:
                copy.wait()

        gate_grad = jnp.zeros((rows, 1), f32)
        for n in range(0, hidden, part):
            x = x_ref[low:high]
            a = jnp.dot(x, wg[:, n : n + part], preferred_element_type=f32)
            up = jnp.dot(x, wu[:, n : n + part], preferred_element_type=f32)
            u = lax.dot_general(
                dy_ref[low:high], wd[n : n + part, :], contract_cols, preferred_element_type=f32
            )
            sig = jax.nn.sigmoid(a)
            active = a * sig
            h = active * up
            gate_grad = gate_grad + jnp.sum(u * h, axis=1, keepdims=True)
            h_ref[low:high, n : n + part] = h.astype(bf16)
            da_ref[low:high, n : n + part] = (u * up * sig * (1.0 + a * (1.0 - sig))).astype(bf16)
            db_ref[low:high, n : n + part] = (u * active).astype(bf16)
        for i in (2, 3, 4):
            out_copy(i, b).start()

        lane = lax.broadcasted_iota(jnp.int32, (block, lanes), 1)
        at = slice(b * block, (b + 1) * block)
        gates = old_gate_ref[at, :] if last else jnp.zeros((block, lanes), f32)
        for p in range(count):
            gates = jnp.where(lane == start + p, gate_grad[p * block : (p + 1) * block], gates)
        if last:
            eight = jnp.broadcast_to(gates[:, None, :], (block, 8, lanes))
            back_ref[at, half : half + 8, :] = eight.astype(bf16)
        else:
            gate_ref[at, :] = gates

        for n in range(0, width, part):
            dx = lax.dot_general(
                da_ref[low:high], wg[n : n + part, :], contract_cols, preferred_element_type=f32
            )
            dx = dx + lax.dot_general(
                db_ref[low:high], wu[n : n + part, :], contract_cols, preferred_element_type=f32
            )
            dx_ref[:, n : n + part] = dx.astype(bf16)

        def narrow(p, carry):
            to = pl.multiple_of(p * sub, sub)
            for s in range(0, block, 2 * sub):
                halves = []
                for d in (0, sub):
                    row = pl.multiple_of(p * block + s + d, sub)
                    halves.append(
                        jnp.concatenate(
                            [
                                dx_ref[pl.ds(row, sub), j * lanes : (j + 1) * lanes]
                                for j in range(chunks)
                            ],
                            axis=0,
                        )
                    )
                tiles = jnp.dot(
                    swap_ref[...], jnp.concatenate(halves, axis=1), preferred_element_type=f32
                ).astype(bf16)
                for d in (0, 1):
                    e = b * block + s + d * sub
                    back_ref[e : e + sub, pl.ds(to, sub), :] = tiles[
                        :, d * lanes : (d + 1) * lanes
                    ].reshape(sub, sub, lanes)
            return carry

        lax.fori_loop(0, count, narrow, 0)

    for b in range(blocks):
        for i in range(5):
            out_copy(i, b).wait()


def expert_rows(wire, wg, wu, wd, start, count, block, carry=None):
    sources = wire.shape[0]
    width, hidden = wg.shape
    mine = sources * count
    last = carry is not None
    total = sources * capacity
    anywhere = pl.BlockSpec(memory_space=pl.ANY)
    high = count * sub + (8 if last else 0)
    back_spec = pl.BlockSpec(
        (pl.Element(sources), pl.Element(high), pl.Element(lanes)),
        lambda i: (0, start * sub, 0),
    )
    out_shape = [
        jax.ShapeDtypeStruct((total, width), bf16),
        jax.ShapeDtypeStruct((total, width), bf16),
        jax.ShapeDtypeStruct((total, hidden), bf16),
        jax.ShapeDtypeStruct((total, hidden), bf16),
        jax.ShapeDtypeStruct((total, hidden), bf16),
        jax.ShapeDtypeStruct((sources, capacity * sub + 8, lanes), bf16),
    ]
    out_specs = [anywhere] * 5 + [back_spec]
    in_specs = [anywhere] * 4
    args = [wire, wg, wu, wd]
    aliases = {}
    if last:
        in_specs += [whole((sources, lanes))] + [anywhere] * 6
        args += [carry[6]] + list(carry[:6])
        aliases = {5 + i: i for i in range(6)}
    else:
        out_specs.append(whole((sources, lanes)))
        out_shape.append(jax.ShapeDtypeStruct((sources, lanes), f32))
    return pl.pallas_call(
        functools.partial(expert_kernel, start, count, block, last),
        grid=(1,),
        in_specs=in_specs,
        out_specs=out_specs,
        out_shape=out_shape,
        scratch_shapes=[
            pltpu.VMEM(wire.shape, bf16),
            pltpu.VMEM((width, hidden), bf16),
            pltpu.VMEM((width, hidden), bf16),
            pltpu.VMEM((hidden, width), bf16),
            pltpu.VMEM((mine, width), bf16),
            pltpu.VMEM((mine, width), bf16),
            pltpu.VMEM((mine, hidden), bf16),
            pltpu.VMEM((mine, hidden), bf16),
            pltpu.VMEM((mine, hidden), bf16),
            pltpu.VMEM((block * count, width), bf16),
            pltpu.VMEM((sub * sub, sub * sub), bf16),
            pltpu.SemaphoreType.DMA((sources // block, 2)),
            pltpu.SemaphoreType.DMA((3,)),
            pltpu.SemaphoreType.DMA((5, sources // block)),
        ],
        input_output_aliases=aliases,
        compiler_params=params(60),
        cost_estimate=pl.CostEstimate(
            flops=10 * mine * width * hidden,
            bytes_accessed=6 * width * hidden + 12 * mine * width,
            transcendentals=mine * hidden,
        ),
        name="expert_rows_last" if last else "expert_rows_first",
    )(*args)


def combine_kernel(code_s_ref, code_ref, num_ref, back_ref, tok_ref, gate_ref, tiles_ref):
    toks, width = tok_ref.shape
    top = code_ref.shape[0]
    chunks = width // lanes
    experts = back_ref.shape[0]

    def one(t, carry):
        total = None
        for k in range(top):
            code = code_s_ref[k, t]
            at = pl.multiple_of((code & 15) << 4, sub)
            row = back_ref[code >> 4, pl.ds(at, sub), :].astype(f32)
            total = row if total is None else total + row
        tiles_ref[t] = total.astype(bf16)
        return carry

    lax.fori_loop(0, toks, one, 0, unroll=4)
    swap = swap_matrix()
    for r in range(0, toks, 2 * sub):
        tiles = jnp.concatenate(
            [tiles_ref[r + d : r + d + sub].reshape(sub * sub, lanes) for d in (0, sub)], axis=1
        )
        flat = jnp.dot(swap, tiles, preferred_element_type=f32).astype(bf16)
        for d in (0, 1):
            for j in range(chunks):
                tok_ref[r + d * sub : r + (d + 1) * sub, j * lanes : (j + 1) * lanes] = flat[
                    j * sub : (j + 1) * sub, d * lanes : (d + 1) * lanes
                ]

    grads = jnp.max(back_ref[:, capacity * sub : capacity * sub + 8, :].astype(f32), axis=1)
    grads = jnp.transpose(grads).astype(bf16)
    gate = num_ref[...].astype(f32) * (1.0 / 256.0)
    expert_at = lax.broadcasted_iota(jnp.int32, (experts, toks), 0)
    place_at = lax.broadcasted_iota(jnp.int32, (lanes, toks), 0)
    found = []
    for k in range(top):
        code = code_ref[k : k + 1, :]
        hit = jnp.where((code >> 4) == expert_at, 1.0, 0.0).astype(bf16)
        rows = jnp.dot(grads, hit, preferred_element_type=f32)
        found.append(jnp.sum(jnp.where((code & 15) == place_at, rows, 0.0), axis=0, keepdims=True))
    gate_ref[...] = (jnp.concatenate(found, axis=0) / gate).astype(bf16)


def combine(code, num, back, toks, width):
    top = code.shape[0]
    vmem = pl.BlockSpec(memory_space=pltpu.VMEM)
    return pl.pallas_call(
        combine_kernel,
        in_specs=[pl.BlockSpec(memory_space=pltpu.SMEM), vmem, vmem, vmem],
        out_specs=[vmem] * 2,
        out_shape=[
            jax.ShapeDtypeStruct((toks, width), bf16),
            jax.ShapeDtypeStruct((top, toks), bf16),
        ],
        scratch_shapes=[pltpu.VMEM((toks, width // lanes, lanes), bf16)],
        compiler_params=params(60),
        name="combine_rows",
    )(code, code, num, back)


def exchange(rows):
    return lax.all_to_all(rows, ("dp", "expert"), split_axis=0, concat_axis=0, tiled=True)


def local(tokens, d_out, expert_ids, gate_num, w_gate, w_up, w_down):
    toks, width = tokens.shape
    experts = lax.axis_size("dp") * lax.axis_size("expert")
    wg, wu, wd = w_gate[0], w_up[0], w_down[0]
    ids, num = expert_ids.T, gate_num.T
    rest = capacity - first_rows
    first, index, scale, code = pack(tokens, d_out, 0, first_rows, experts, ids, num)
    (second,) = pack(tokens, d_out, first_rows, rest, experts, tables=(index, scale))
    first, second = exchange(first), exchange(second)
    part = expert_rows(first, wg, wu, wd, 0, first_rows, 64)
    rows_x, rows_dy, h, da, db, back = expert_rows(second, wg, wu, wd, first_rows, rest, 128, part)
    back = exchange(back)
    grad_gate = lax.dot_general(rows_x, da, contract_rows, preferred_element_type=f32).astype(bf16)
    grad_up = lax.dot_general(rows_x, db, contract_rows, preferred_element_type=f32).astype(bf16)
    grad_down = lax.dot_general(h, rows_dy, contract_rows, preferred_element_type=f32).astype(bf16)
    d_tokens, d_gate = combine(code, num, back, toks, width)
    return (d_tokens, d_gate.T, grad_gate[None], grad_up[None], grad_down[None])


def solution(mesh):
    rows = P(("dp", "expert"), None)
    blocks = P(("dp", "expert"), None, None)
    return jax.shard_map(
        local,
        mesh=mesh,
        in_specs=(rows, rows, rows, rows, blocks, blocks, blocks),
        out_specs=(rows, rows, blocks, blocks, blocks),
        check_vma=False,
    )
```

time: 495 us -> 239 us (0.48)
  the two profiles are of different devices: /device:TPU:90 before, /device:TPU:1 now
where the time goes in v1:
time: 239 us
  waiting for transfers between devices  122 us (51%)
  Pallas kernels  65.1 us (27%)
  starting transfers between devices  29.8 us (12%)
  matrix products  19.6 us (8%)
    all_to_all x3, waiting for transfers between devices, exchange(): lax.all_to_all(rows, ('dp', 'expert'), split_axis=0, concat_axis=0, tiled...  122 us
    pallas_call x2, Pallas kernels, expert_rows(): pl.pallas_call(functools.partial(expert_kernel, start, count, block, last...  44.4 us
    all_to_all x3, starting transfers between devices, exchange(): lax.all_to_all(rows, ('dp', 'expert'), split_axis=0, concat_axis=0, tiled...  29.8 us
    pallas_call x2, Pallas kernels, pack(): pl.pallas_call(body, grid=(experts // group,), in_specs=in_specs, out_spe...  13.8 us
    dot_general x1, matrix products, local(): lax.dot_general(rows_x, da, contract_rows, preferred_element_type=f32)  8.26 us
    pallas_call x1, Pallas kernels, combine(): pl.pallas_call(combine_kernel, in_specs=[pl.BlockSpec(memory_space=pltpu....  6.89 us
    dot_general x1, matrix products, local(): lax.dot_general(rows_x, db, contract_rows, preferred_element_type=f32)  5.74 us
    dot_general x1, matrix products, local(): lax.dot_general(h, rows_dy, contract_rows, preferred_element_type=f32)  5.64 us
  transfers between devices with their start and end apart: 3, of which 2 were waited for; matrix products, arithmetic and copies ran while one was open for 8% of the time, Pallas kernels for 16%

profile of v1, /device:TPU:1, one launch (start us, length us, event | category | flops | bytes accessed | tf_op | source)
XLA Modules:
  0.0 239.0 jit_solution(4057612483173367399)
XLA Ops:
  0.6 8.2 %pack_first.1 = (bf16[128,224,128]{2,1,0:T(8,128)(2,1)}, s32[16,128]{1,0:T(8,128)}, f32[16,128]{1,0:T(8,128)}, s32[8,128]{1,0:T(8,128)}) custom-call(s32[8,128]{1,0:T(8,128)} %bitcast.30, s32[8,128]{1,0:T(8,128)} %bitcast.28, bf16[128,2048]{1,0:T(8,128)(2,1)} %tok_ref.3, bf16[128,2048]{1,0:T(8,128)(2,1)} %dy_ref.3), custom_call_target="tpu_custom_call" | custom-call | bytes 7340032 | tf_op jit(solution)/shard_map/pack_first/pallas_call | solution.py:175
  8.9 11.9 %all-to-all-start.1 = ((bf16[128,224,128]{2,1,0:T(8,128)(2,1)}), bf16[128,224,128]{2,1,0:T(8,128)(2,1)}, u32[]{:S(2)}, u32[]{:S(2)}) async-start(bf16[128,224,128]{2,1,0:T(8,128)(2,1)} %get-tuple-element.27), calls=%async_computation.1 | async-start | bytes 14680064 | tf_op jit(solution)/shard_map/all_to_all | solution.py:469
  20.8 5.6 %pack_rest.1 = bf16[128,64,128]{2,1,0:T(8,128)(2,1)} custom-call(s32[16,128]{1,0:T(8,128)} %get-tuple-element.25.index_ref, f32[16,128]{1,0:T(8,128)} %get-tuple-element.26.scale_ref, bf16[128,2048]{1,0:T(8,128)(2,1)} %tok_ref.3, bf16[128,2048]{1,0:T(8,128)(2,1)} %dy_ref.3), custom_call_target="tpu_custom_call" | custom-call | bytes 2097152 | tf_op jit(solution)/shard_map/pack_rest/pallas_call | solution.py:175
  26.4 81.1 %all-to-all-done.1.refs_0_ = bf16[128,224,128]{2,1,0:T(8,128)(2,1)} async-done(((bf16[128,224,128]{2,1,0:T(8,128)(2,1)}), bf16[128,224,128]{2,1,0:T(8,128)(2,1)}, u32[]{:S(2)}, u32[]{:S(2)}) %all-to-all-start.1) | async-done | bytes 7340064 | tf_op jit(solution)/shard_map/all_to_all | solution.py:469
  107.5 7.7 %all-to-all-start = ((bf16[128,64,128]{2,1,0:T(8,128)(2,1)}), bf16[128,64,128]{2,1,0:T(8,128)(2,1)S(1)}, u32[]{:S(2)}, u32[]{:S(2)}) async-start(bf16[128,64,128]{2,1,0:T(8,128)(2,1)} %pack_rest.1), calls=%async_computation | async-start | bytes 4194304 | tf_op jit(solution)/shard_map/all_to_all | solution.py:469
  115.2 32.3 %expert_rows_first.1 = (bf16[1152,2048]{1,0:T(8,128)(2,1)}, bf16[1152,2048]{1,0:T(8,128)(2,1)}, bf16[1152,768]{1,0:T(8,128)(2,1)}, bf16[1152,768]{1,0:T(8,128)(2...) custom-call(bf16[128,224,128]{2,1,0:T(8,128)(2,1)} %all-to-all-done.1.refs_0_, ...), custom_call_target="tpu_custom_call" | custom-call | flops 14092861440 | bytes 31457280 | tf_op jit(solution)/shard_map/expert_rows_first/pallas_call | solution.py:375
  147.5 0.0 all-to-all-done.refs_0_
  147.5 0.0 copy-start
  147.5 1.3 copy-done
  148.8 12.1 %expert_rows_last.1 = (bf16[1152,2048]{1,0:T(8,128)(2,1)}, bf16[1152,2048]{1,0:T(8,128)(2,1)}, bf16[1152,768]{1,0:T(8,128)(2,1)}, bf16[1152,768]{1,0:T(8,128)(2,...) custom-call(bf16[128,64,128]{2,1,0:T(8,128)(2,1)} %copy-done, ...), custom_call_target="tpu_custom_call", output_to_operand_aliasing={{0}: (5, {}), {1}: (6, {}), {2}: (7, {}), {3}: (8, {}), {4}... | custom-call | flops 4026531840 | bytes 15728640 | tf_op jit(solution)/shard_map/expert_rows_last/pallas_call | solution.py:375
  160.9 0.0 copy-start.2
  160.9 0.0 slice-start
  160.9 10.2 %all-to-all-start.2 = ((bf16[128,152,128]{2,1,0:T(8,128)(2,1)}), bf16[128,152,128]{2,1,0:T(8,128)(2,1)}, u32[]{:S(2)}, u32[]{:S(2)}) async-start(bf16[128,152,128]{2,1,0:T(8,128)(2,1)} %get-tuple-element.35), calls=%async_computation.2 | async-start | bytes 9961472 | tf_op jit(solution)/shard_map/all_to_all | solution.py:469
  171.1 0.0 copy-done.2
  171.2 0.0 slice-start.1
  171.2 0.0 copy-start.3
  171.2 0.0 slice-start.2
  171.2 8.3 %fusion = bf16[1,2048,768]{2,1,0:T(8,128)(2,1)} fusion(bf16[1152,2048]{1,0:T(8,128)(2,1)} %get-tuple-element.38, bf16[1152,768]{1,0:T(8,128)(2,1)S(1)} %copy-done.2), kind=kOutput, calls=%fused_computation.3 | convolution fusion | flops 3625451520 | bytes 9633792 | tf_op jit(solution)/shard_map/dot_general | solution.py:484
  179.4 0.0 slice-done
  179.5 0.0 slice-done.1
  179.5 0.0 copy-done.3
  179.5 0.0 slice-start.3
  179.5 0.0 copy-start.1
  179.5 5.7 %fusion.1 = bf16[1,2048,768]{2,1,0:T(8,128)(2,1)} fusion(bf16[1152,2048]{1,0:T(8,128)(2,1)S(1)} %bitcast.19, bf16[1152,768]{1,0:T(8,128)(2,1)S(1)} %copy-done.3), kind=kOutput, calls=%fused_computation.4 | convolution fusion | flops 3625451520 | bytes 9633792 | tf_op jit(solution)/shard_map/dot_general | solution.py:485
  185.2 0.0 slice-done.2
  185.2 0.0 slice-done.3
  185.2 0.0 copy-done.1
  185.2 5.6 %fusion.2 = bf16[1,768,2048]{2,1,0:T(8,128)(2,1)} fusion(bf16[1152,768]{1,0:T(8,128)(2,1)S(1)} %copy-done.1, bf16[1152,2048]{1,0:T(8,128)(2,1)S(1)} %bitcast.21), kind=kOutput, calls=%fused_computation.5 | convolution fusion | flops 3625451520 | bytes 9633792 | tf_op jit(solution)/shard_map/dot_general | solution.py:486
  190.9 41.2 %all-to-all-done.2.back_ref = bf16[128,152,128]{2,1,0:T(8,128)(2,1)} async-done(((bf16[128,152,128]{2,1,0:T(8,128)(2,1)}), bf16[128,152,128]{2,1,0:T(8,128)(2,1)}, u32[]{:S(2)}, u32[]{:S(2)}) %all-to-all-start.2) | async-done | bytes 4980768 | tf_op jit(solution)/shard_map/all_to_all | solution.py:469
  232.1 6.9 %combine_rows.1 = (bf16[128,2048]{1,0:T(8,128)(2,1)}, bf16[8,128]{1,0:T(8,128)(2,1)}) custom-call(s32[8,128]{1,0:T(8,128)} %get-tuple-element.24.code_s_ref.code_ref, s32[8,128]{1,0:T(8,128)} %get-tuple-element.24.code_s_ref.code_ref, s32[8,128]{1,0:T(8,128)} %bitcast.29, bf16[128,152,128]{2,1,0:T(8,128)(2,1)} %all-to-all-done.2.back_ref), custom_call_target="tpu_custom_call" | custom-call | tf_op jit(solution)/shard_map/combine_rows/pallas_call | solution.py:454
  (2 shorter events, 0.0 us)
Async XLA Ops:
  8.9 98.6 %all-to-all-start.1 = ((bf16[128,224,128]{2,1,0:T(8,128)(2,1)}), bf16[128,224,128]{2,1,0:T(8,128)(2,1)}, u32[]{:S(2)}, u32[]{:S(2)}) async-start(bf16[128,224,128]{2,1,0:T(8,128)(2,1)} %get-tuple-element.27), calls=%async_computation.1 | async-start | bytes 14680064 | tf_op jit(solution)/shard_map/all_to_all | solution.py:469
  107.5 40.0 %all-to-all-start = ((bf16[128,64,128]{2,1,0:T(8,128)(2,1)}), bf16[128,64,128]{2,1,0:T(8,128)(2,1)S(1)}, u32[]{:S(2)}, u32[]{:S(2)}) async-start(bf16[128,64,128]{2,1,0:T(8,128)(2,1)} %pack_rest.1), calls=%async_computation | async-start | bytes 4194304 | tf_op jit(solution)/shard_map/all_to_all | solution.py:469
  147.5 1.3 copy-start
  160.9 10.2 %copy-start.2 = (bf16[1152,768]{1,0:T(8,128)(2,1)S(1)}, bf16[1152,768]{1,0:T(8,128)(2,1)}, u32[]{:S(2)}) copy-start(bf16[1152,768]{1,0:T(8,128)(2,1)} %get-tuple-element.39) | copy-start | bytes 5308420
  160.9 18.5 %slice-start = ((s8[4718592]{0:T(1024)(128)(4,1)}), s8[524288]{0:T(1024)(128)(4,1)S(1)}, s32[]{:S(2)}) async-start(s8[4718592]{0:T(1024)(128)(4,1)} %bitcast.18), calls=%async_computation.3 | async-start | bytes 1048576
  160.9 71.2 %all-to-all-start.2 = ((bf16[128,152,128]{2,1,0:T(8,128)(2,1)}), bf16[128,152,128]{2,1,0:T(8,128)(2,1)}, u32[]{:S(2)}, u32[]{:S(2)}) async-start(bf16[128,152,128]{2,1,0:T(8,128)(2,1)} %get-tuple-element.35), calls=%async_computation.2 | async-start | bytes 9961472 | tf_op jit(solution)/shard_map/all_to_all | solution.py:469
  171.2 8.3 %slice-start.1 = ((s8[4718592]{0:T(1024)(128)(4,1)}), s8[4194304]{0:T(1024)(128)(4,1)S(1)}, s32[]{:S(2)}) async-start(s8[4718592]{0:T(1024)(128)(4,1)} %bitcast.18), calls=%async_computation.4 | async-start | bytes 8388608
  171.2 8.3 %copy-start.3 = (bf16[1152,768]{1,0:T(8,128)(2,1)S(1)}, bf16[1152,768]{1,0:T(8,128)(2,1)}, u32[]{:S(2)}) copy-start(bf16[1152,768]{1,0:T(8,128)(2,1)} %get-tuple-element.40) | copy-start | bytes 5308420
  171.2 14.1 %slice-start.2 = ((s8[4718592]{0:T(1024)(128)(4,1)}), s8[4194304]{0:T(1024)(128)(4,1)S(1)}, s32[]{:S(2)}) async-start(s8[4718592]{0:T(1024)(128)(4,1)} %bitcast.20), calls=%async_computation.5 | async-start | bytes 8388608
  179.5 5.8 %slice-start.3 = ((s8[4718592]{0:T(1024)(128)(4,1)}), s8[524288]{0:T(1024)(128)(4,1)S(1)}, s32[]{:S(2)}) async-start(s8[4718592]{0:T(1024)(128)(4,1)} %bitcast.20), calls=%async_computation.6 | async-start | bytes 1048576
  179.5 5.8 %copy-start.1 = (bf16[1152,768]{1,0:T(8,128)(2,1)S(1)}, bf16[1152,768]{1,0:T(8,128)(2,1)}, u32[]{:S(2)}) copy-start(bf16[1152,768]{1,0:T(8,128)(2,1)} %get-tuple-element.41) | copy-start | bytes 5308420

commit v2 on v1

--- a/solution.py
+++ b/solution.py
@@ -96,73 +96,81 @@
     wide_to_tiles(swap, dy_ref, chunks, put_dy)
 
 
-def fill_rows(start, count, index_ref, scale_ref, tok_tiles, dy_tiles, out_ref):
-    group = out_ref.shape[0]
-    first = pl.program_id(0) * group
+def fill_rows(start, count, index_ref, scale_ref, tok_tiles, dy_tiles, buffer, out_hbm, sems):
+    experts = buffer.shape[0]
+    groups = sems.shape[0]
+    group = experts // groups
+
+    def out_copy(g):
+        at = slice(g * group, (g + 1) * group)
+        return pltpu.make_async_copy(buffer.at[at], out_hbm.at[at], sems.at[g])
 
     def one(e, carry):
         for p in range(count):
-            token = index_ref[start + p, first + e]
-            scale = scale_ref[start + p, first + e]
-            out_ref[e, p * sub : (p + 1) * sub, :] = tok_tiles[token]
+            token = index_ref[start + p, e]
+            scale = scale_ref[start + p, e]
+            buffer[e, p * sub : (p + 1) * sub, :] = tok_tiles[token]
             at = (count + p) * sub
-            out_ref[e, at : at + sub, :] = (dy_tiles[token] * scale).astype(bf16)
+            buffer[e, at : at + sub, :] = (dy_tiles[token] * scale).astype(bf16)
         return carry
 
-    lax.fori_loop(0, group, one, 0)
+    for g in range(groups):
+        lax.fori_loop(g * group, (g + 1) * group, one, 0, unroll=2)
+        out_copy(g).start()
+    for g in range(groups):
+        out_copy(g).wait()
 
 
 def pack_first_kernel(
     start, count, ids_ref, num_ref, tok_ref, dy_ref,
-    out_ref, index_ref, scale_ref, code_ref, tok_tiles, dy_tiles, index_s, scale_s, sems,
+    out_hbm, index_ref, scale_ref, code_ref,
+    tok_tiles, dy_tiles, buffer, out_sems, index_s, scale_s, sems,
 ):
-    @pl.when(pl.program_id(0) == 0)
-    def _():
-        index, scale, code = spread_tables(ids_ref[...], num_ref[...], index_ref.shape[1])
-        index_ref[...] = index
-        scale_ref[...] = scale
-        code_ref[...] = code
-        one = pltpu.make_async_copy(index_ref, index_s, sems.at[0])
-        two = pltpu.make_async_copy(scale_ref, scale_s, sems.at[1])
-        one.start()
-        two.start()
-        make_tiles(tok_ref, dy_ref, tok_tiles, dy_tiles)
-        one.wait()
-        two.wait()
-
-    fill_rows(start, count, index_s, scale_s, tok_tiles, dy_tiles, out_ref)
+    index, scale, code = spread_tables(ids_ref[...], num_ref[...], index_ref.shape[1])
+    index_ref[...] = index
+    scale_ref[...] = scale
+    code_ref[...] = code
+    one = pltpu.make_async_copy(index_ref, index_s, sems.at[0])
+    two = pltpu.make_async_copy(scale_ref, scale_s, sems.at[1])
+    one.start()
+    two.start()
+    make_tiles(tok_ref, dy_ref, tok_tiles, dy_tiles)
+    one.wait()
+    two.wait()
+    fill_rows(start, count, index_s, scale_s, tok_tiles, dy_tiles, buffer, out_hbm, out_sems)
 
 
 def pack_rest_kernel(
-    start, count, index_ref, scale_ref, tok_ref, dy_ref, out_ref, tok_tiles, dy_tiles
+    start, count, index_ref, scale_ref, tok_ref, dy_ref,
+    out_hbm, tok_tiles, dy_tiles, buffer, out_sems,
 ):
-    @pl.when(pl.program_id(0) == 0)
-    def _():
-        make_tiles(tok_ref, dy_ref, tok_tiles, dy_tiles)
-
-    fill_rows(start, count, index_ref, scale_ref, tok_tiles, dy_tiles, out_ref)
+    make_tiles(tok_ref, dy_ref, tok_tiles, dy_tiles)
+    fill_rows(start, count, index_ref, scale_ref, tok_tiles, dy_tiles, buffer, out_hbm, out_sems)
 
 
 def pack(tokens, d_out, start, count, experts, ids=None, num=None, tables=None):
     toks, width = tokens.shape
     chunks = width // lanes
-    group = 16
-    out_shape = [jax.ShapeDtypeStruct((experts, 2 * count * sub, lanes), bf16)]
-    out_specs = [pl.BlockSpec((group, 2 * count * sub, lanes), lambda i: (i, 0, 0))]
+    wire = (experts, 2 * count * sub, lanes)
+    out_shape = [jax.ShapeDtypeStruct(wire, bf16)]
+    out_specs = [pl.BlockSpec(memory_space=pl.ANY)]
     scratch = [
         pltpu.VMEM((toks, chunks, lanes), bf16),
         pltpu.VMEM((toks, chunks, lanes), f32),
+        pltpu.VMEM(wire, bf16),
+        pltpu.SemaphoreType.DMA((8,)),
     ]
+    vmem = pl.BlockSpec(memory_space=pltpu.VMEM)
     if tables is None:
         body = functools.partial(pack_first_kernel, start, count)
         args = (ids, num, tokens, d_out)
-        in_specs = [whole(a.shape) for a in args]
+        in_specs = [vmem] * 4
         out_shape += [
             jax.ShapeDtypeStruct((sub, experts), jnp.int32),
             jax.ShapeDtypeStruct((sub, experts), f32),
             jax.ShapeDtypeStruct(ids.shape, jnp.int32),
         ]
-        out_specs += [whole(o.shape) for o in out_shape[1:]]
+        out_specs += [vmem] * 3
         scratch += [
             pltpu.SMEM((sub, experts), jnp.int32),
             pltpu.SMEM((sub, experts), f32),
@@ -171,10 +179,9 @@
     else:
         body = functools.partial(pack_rest_kernel, start, count)
         args = (*tables, tokens, d_out)
-        in_specs = [pl.BlockSpec(memory_space=pltpu.SMEM)] * 2 + [whole(tokens.shape)] * 2
+        in_specs = [pl.BlockSpec(memory_space=pltpu.SMEM)] * 2 + [vmem] * 2
     return pl.pallas_call(
         body,
-        grid=(experts // group,),
         in_specs=in_specs,
         out_specs=out_specs,
         out_shape=out_shape,
@@ -188,7 +195,7 @@
 
 
 def expert_kernel(start, count, block, last, *refs):
-    (wire_hbm, wg_hbm, wu_hbm, wd_hbm) = refs[:4]
+    (wire_hbm, wg, wu_hbm, wd_hbm) = refs[:4]
     refs = refs[4:]
     if last:
         old_gate_ref = refs[0]
@@ -199,8 +206,8 @@
     if not last:
         gate_ref = refs[0]
         refs = refs[1:]
-    (wire, wg, wu, wd, x_ref, dy_ref, h_ref, da_ref, db_ref, dx_ref, swap_ref) = refs[:11]
-    (wire_sem, weight_sem, out_sem) = refs[11:]
+    (wire, wu, wd, x_ref, dy_ref, h_ref, da_ref, db_ref, dx_ref, swap_ref) = refs[:10]
+    (wire_sem, weight_sem, out_sem) = refs[10:]
     sources = wire_hbm.shape[0]
     blocks = sources // block
     rows = block * count
@@ -215,7 +222,7 @@
 
     weights = [
         pltpu.make_async_copy(src, dst, weight_sem.at[i])
-        for i, (src, dst) in enumerate(((wg_hbm, wg), (wu_hbm, wu), (wd_hbm, wd)))
+        for i, (src, dst) in enumerate(((wu_hbm, wu), (wd_hbm, wd)))
     ]
 
     def out_copy(i, b):
@@ -227,9 +234,8 @@
 
     wire_copy(0, 0).start()
     weights[0].start()
+    wire_copy(0, 1).start()
     weights[1].start()
-    wire_copy(0, 1).start()
-    weights[2].start()
     for b in range(1, blocks):
         wire_copy(b, 0).start()
         wire_copy(b, 1).start()
@@ -257,13 +263,17 @@
                         ]
             return carry
 
-        lax.fori_loop(0, count, step, 0)
+        lax.fori_loop(0, count, step, 0, unroll=True)
 
     for b in range(blocks):
         low, high = b * rows, (b + 1) * rows
         wire_copy(b, 0).wait()
         widen(b, 0, x_ref)
         out_copy(0, b).start()
+        gates_in = [
+            jnp.dot(x_ref[low:high], wg[:, n : n + part], preferred_element_type=f32)
+            for n in range(0, hidden, part)
+        ]
         wire_copy(b, 1).wait()
         widen(b, 1, dy_ref)
         out_copy(1, b).start()
@@ -274,7 +284,7 @@
         gate_grad = jnp.zeros((rows, 1), f32)
         for n in range(0, hidden, part):
             x = x_ref[low:high]
-            a = jnp.dot(x, wg[:, n : n + part], preferred_element_type=f32)
+            a = gates_in[n // part]
             up = jnp.dot(x, wu[:, n : n + part], preferred_element_type=f32)
             u = lax.dot_general(
                 dy_ref[low:high], wd[n : n + part, :], contract_cols, preferred_element_type=f32
@@ -334,7 +344,7 @@
                     ].reshape(sub, sub, lanes)
             return carry
 
-        lax.fori_loop(0, count, narrow, 0)
+        lax.fori_loop(0, count, narrow, 0, unroll=True)
 
     for b in range(blocks):
         for i in range(5):
@@ -347,7 +357,7 @@
     mine = sources * count
     last = carry is not None
     total = sources * capacity
-    anywhere = pl.BlockSpec(memory_space=pl.ANY)
+    anywhere = pl.BlockSpec(memory_space=pltpu.HBM)
     high = count * sub + (8 if last else 0)
     back_spec = pl.BlockSpec(
         (pl.Element(sources), pl.Element(high), pl.Element(lanes)),
@@ -362,8 +372,8 @@
         jax.ShapeDtypeStruct((sources, capacity * sub + 8, lanes), bf16),
     ]
     out_specs = [anywhere] * 5 + [back_spec]
-    in_specs = [anywhere] * 4
-    args = [wire, wg, wu, wd]
+    in_specs = [anywhere, pl.BlockSpec(memory_space=pltpu.VMEM), anywhere, anywhere]
+    args = [wire, pltpu.with_memory_space_constraint(wg, pltpu.VMEM), wu, wd]
     aliases = {}
     if last:
         in_specs += [whole((sources, lanes))] + [anywhere] * 6
@@ -381,7 +391,6 @@
         scratch_shapes=[
             pltpu.VMEM(wire.shape, bf16),
             pltpu.VMEM((width, hidden), bf16),
-            pltpu.VMEM((width, hidden), bf16),
             pltpu.VMEM((hidden, width), bf16),
             pltpu.VMEM((mine, width), bf16),
             pltpu.VMEM((mine, width), bf16),
@@ -391,7 +400,7 @@
             pltpu.VMEM((block * count, width), bf16),
             pltpu.VMEM((sub * sub, sub * sub), bf16),
             pltpu.SemaphoreType.DMA((sources // block, 2)),
-            pltpu.SemaphoreType.DMA((3,)),
+            pltpu.SemaphoreType.DMA((2,)),
             pltpu.SemaphoreType.DMA((5, sources // block)),
         ],
         input_output_aliases=aliases,
@@ -421,7 +430,7 @@
         tiles_ref[t] = total.astype(bf16)
         return carry
 
-    lax.fori_loop(0, toks, one, 0, unroll=4)
+    lax.fori_loop(0, toks, one, 0, unroll=8)
     swap = swap_matrix()
     for r in range(0, toks, 2 * sub):
         tiles = jnp.concatenate(

time: 239 us -> 229 us (0.958)
  Pallas kernels: 65.1 us -> 51.8 us
  waiting for transfers between devices: 122 us -> 130 us
  starting transfers between devices: 29.8 us -> 25.8 us
    pallas_call x2, Pallas kernels: 44.4 us -> 34.6 us  [expert_rows(): pl.pallas_call(functools.partial(expert_kernel, start, count, block, last...]
    all_to_all x3, waiting for transfers between devices: 122 us -> 130 us  [exchange(): lax.all_to_all(rows, ('dp', 'expert'), split_axis=0, concat_axis=0, tiled...]
    all_to_all x3, starting transfers between devices: 29.8 us -> 25.8 us  [exchange(): lax.all_to_all(rows, ('dp', 'expert'), split_axis=0, concat_axis=0, tiled...]
    pallas_call x2, Pallas kernels: 13.8 us -> 10.3 us  [pack(): pl.pallas_call(body, in_specs=in_specs, out_specs=out_specs, out_shape=ou...]
  transfers between devices with their start and end apart: 3 -> 3, of which waited for: 2 -> 3; matrix products, arithmetic and copies ran while one was open for 8% -> 9% of each run, Pallas kernels for 16% -> 12%
where the time goes in v2:
time: 229 us; the launch traced here: 228 us
  waiting for transfers between devices  130 us (57%)
  Pallas kernels  51.8 us (23%)
  starting transfers between devices  25.8 us (11%)
  matrix products  19.6 us (9%)
    all_to_all x3, waiting for transfers between devices, exchange(): lax.all_to_all(rows, ('dp', 'expert'), split_axis=0, concat_axis=0, tiled...  130 us
    pallas_call x2, Pallas kernels, expert_rows(): pl.pallas_call(functools.partial(expert_kernel, start, count, block, last...  34.6 us
    all_to_all x3, starting transfers between devices, exchange(): lax.all_to_all(rows, ('dp', 'expert'), split_axis=0, concat_axis=0, tiled...  25.8 us
    pallas_call x2, Pallas kernels, pack(): pl.pallas_call(body, in_specs=in_specs, out_specs=out_specs, out_shape=ou...  10.3 us
    dot_general x1, matrix products, local(): lax.dot_general(rows_x, da, contract_rows, preferred_element_type=f32)  8.27 us
    pallas_call x1, Pallas kernels, combine(): pl.pallas_call(combine_kernel, in_specs=[pl.BlockSpec(memory_space=pltpu....  6.87 us
    dot_general x1, matrix products, local(): lax.dot_general(rows_x, db, contract_rows, preferred_element_type=f32)  5.72 us
    dot_general x1, matrix products, local(): lax.dot_general(h, rows_dy, contract_rows, preferred_element_type=f32)  5.64 us
  transfers between devices with their start and end apart: 3, of which 3 were waited for; matrix products, arithmetic and copies ran while one was open for 9% of the time, Pallas kernels for 12%

profile of v2, /device:TPU:1, one launch (start us, length us, event | category | flops | bytes accessed | tf_op | source)
XLA Modules:
  0.0 228.3 jit_solution(2553805013191906811)
XLA Ops:
  0.6 6.6 %pack_first.1 = (bf16[128,224,128]{2,1,0:T(8,128)(2,1)}, s32[16,128]{1,0:T(8,128)}, f32[16,128]{1,0:T(8,128)}, s32[8,128]{1,0:T(8,128)}) custom-call(s32[8,128]{1,0:T(8,128)} %bitcast.30, s32[8,128]{1,0:T(8,128)} %bitcast.28, bf16[128,2048]{1,0:T(8,128)(2,1)} %tok_ref.3, bf16[128,2048]{1,0:T(8,128)(2,1)} %dy_ref.3), custom_call_target="tpu_custom_call" | custom-call | bytes 7340032 | tf_op jit(solution)/shard_map/pack_first/pallas_call | solution.py:183
  7.2 11.9 %all-to-all-start.1 = ((bf16[128,224,128]{2,1,0:T(8,128)(2,1)}), bf16[128,224,128]{2,1,0:T(8,128)(2,1)}, u32[]{:S(2)}, u32[]{:S(2)}) async-start(bf16[128,224,128]{2,1,0:T(8,128)(2,1)} %get-tuple-element.27), calls=%async_computation.1 | async-start | bytes 14680064 | tf_op jit(solution)/shard_map/all_to_all | solution.py:478
  19.2 0.0 copy-start
  19.2 3.7 %pack_rest.1 = bf16[128,64,128]{2,1,0:T(8,128)(2,1)} custom-call(s32[16,128]{1,0:T(8,128)} %get-tuple-element.25.index_ref, f32[16,128]{1,0:T(8,128)} %get-tuple-element.26.scale_ref, bf16[128,2048]{1,0:T(8,128)(2,1)} %tok_ref.3, bf16[128,2048]{1,0:T(8,128)(2,1)} %dy_ref.3), custom_call_target="tpu_custom_call" | custom-call | bytes 2097152 | tf_op jit(solution)/shard_map/pack_rest/pallas_call | solution.py:183
  22.8 83.0 %all-to-all-done.1.refs_0_ = bf16[128,224,128]{2,1,0:T(8,128)(2,1)} async-done(((bf16[128,224,128]{2,1,0:T(8,128)(2,1)}), bf16[128,224,128]{2,1,0:T(8,128)(2,1)}, u32[]{:S(2)}, u32[]{:S(2)}) %all-to-all-start.1) | async-done | bytes 7340064 | tf_op jit(solution)/shard_map/all_to_all | solution.py:478
  105.9 8.3 %all-to-all-start = ((bf16[128,64,128]{2,1,0:T(8,128)(2,1)}), bf16[128,64,128]{2,1,0:T(8,128)(2,1)}, u32[]{:S(2)}, u32[]{:S(2)}) async-start(bf16[128,64,128]{2,1,0:T(8,128)(2,1)} %pack_rest.1), calls=%async_computation | async-start | bytes 4194304 | tf_op jit(solution)/shard_map/all_to_all | solution.py:478
  114.2 0.0 copy-done
  114.2 24.2 %expert_rows_first.1 = (bf16[1152,2048]{1,0:T(8,128)(2,1)}, bf16[1152,2048]{1,0:T(8,128)(2,1)}, bf16[1152,768]{1,0:T(8,128)(2,1)}, bf16[1152,768]{1,0:T(8,128)(2...) custom-call(bf16[128,224,128]{2,1,0:T(8,128)(2,1)} %all-to-all-done.1.refs_0_, ...), custom_call_target="tpu_custom_call" | custom-call | flops 14092861440 | bytes 31457280 | tf_op jit(solution)/shard_map/expert_rows_first/pallas_call | solution.py:385
  138.4 5.8 %all-to-all-done.refs_0_ = bf16[128,64,128]{2,1,0:T(8,128)(2,1)} async-done(((bf16[128,64,128]{2,1,0:T(8,128)(2,1)}), bf16[128,64,128]{2,1,0:T(8,128)(2,1)}, u32[]{:S(2)}, u32[]{:S(2)}) %all-to-all-start) | async-done | bytes 2097184 | tf_op jit(solution)/shard_map/all_to_all | solution.py:478
  144.2 10.5 %expert_rows_last.1 = (bf16[1152,2048]{1,0:T(8,128)(2,1)}, bf16[1152,2048]{1,0:T(8,128)(2,1)}, bf16[1152,768]{1,0:T(8,128)(2,1)}, bf16[1152,768]{1,0:T(8,128)(2,...) custom-call(bf16[128,64,128]{2,1,0:T(8,128)(2,1)} %all-to-all-done.r, ...), custom_call_target="tpu_custom_call", output_to_operand_aliasing={{0}: (5, {}), {1}: (6, {}), {2}: (7, {}), {3}: (8, {}), {4}... | custom-call | flops 4026531840 | bytes 15728640 | tf_op jit(solution)/shard_map/expert_rows_last/pallas_call | solution.py:385
  154.7 0.0 copy-start.2
  154.7 0.0 slice-start
  154.7 5.6 %all-to-all-start.2 = ((bf16[128,152,128]{2,1,0:T(8,128)(2,1)}), bf16[128,152,128]{2,1,0:T(8,128)(2,1)}, u32[]{:S(2)}, u32[]{:S(2)}) async-start(bf16[128,152,128]{2,1,0:T(8,128)(2,1)} %get-tuple-element.35), calls=%async_computation.2 | async-start | bytes 9961472 | tf_op jit(solution)/shard_map/all_to_all | solution.py:478
  160.3 0.0 copy-done.2
  160.3 0.0 slice-start.1
  160.3 0.0 copy-start.3
  160.3 0.0 slice-start.2
  160.3 8.3 %fusion = bf16[1,2048,768]{2,1,0:T(8,128)(2,1)} fusion(bf16[1152,2048]{1,0:T(8,128)(2,1)} %get-tuple-element.38, bf16[1152,768]{1,0:T(8,128)(2,1)S(1)} %copy-done.2), kind=kOutput, calls=%fused_computation.3 | convolution fusion | flops 3625451520 | bytes 9633792 | tf_op jit(solution)/shard_map/dot_general | solution.py:493
  168.6 0.0 slice-done
  168.6 0.0 slice-done.1
  168.6 0.0 copy-done.3
  168.6 0.0 slice-start.3
  168.6 0.0 copy-start.1
  168.6 5.7 %fusion.1 = bf16[1,2048,768]{2,1,0:T(8,128)(2,1)} fusion(bf16[1152,2048]{1,0:T(8,128)(2,1)S(1)} %bitcast.21, bf16[1152,768]{1,0:T(8,128)(2,1)S(1)} %copy-done.3), kind=kOutput, calls=%fused_computation.4 | convolution fusion | flops 3625451520 | bytes 9633792 | tf_op jit(solution)/shard_map/dot_general | solution.py:494
  174.3 0.0 slice-done.2
  174.3 0.0 slice-done.3
  174.3 0.0 copy-done.1
  174.4 5.6 %fusion.2 = bf16[1,768,2048]{2,1,0:T(8,128)(2,1)} fusion(bf16[1152,768]{1,0:T(8,128)(2,1)S(1)} %copy-done.1, bf16[1152,2048]{1,0:T(8,128)(2,1)S(1)} %bitcast.23), kind=kOutput, calls=%fused_computation.5 | convolution fusion | flops 3625451520 | bytes 9633792 | tf_op jit(solution)/shard_map/dot_general | solution.py:495
  180.0 41.4 %all-to-all-done.2.back_ref = bf16[128,152,128]{2,1,0:T(8,128)(2,1)} async-done(((bf16[128,152,128]{2,1,0:T(8,128)(2,1)}), bf16[128,152,128]{2,1,0:T(8,128)(2,1)}, u32[]{:S(2)}, u32[]{:S(2)}) %all-to-all-start.2) | async-done | bytes 4980768 | tf_op jit(solution)/shard_map/all_to_all | solution.py:478
  221.4 6.9 %combine_rows.1 = (bf16[128,2048]{1,0:T(8,128)(2,1)}, bf16[8,128]{1,0:T(8,128)(2,1)}) custom-call(s32[8,128]{1,0:T(8,128)} %get-tuple-element.24.code_s_ref.code_ref, s32[8,128]{1,0:T(8,128)} %get-tuple-element.24.code_s_ref.code_ref, s32[8,128]{1,0:T(8,128)} %bitcast.29, bf16[128,152,128]{2,1,0:T(8,128)(2,1)} %all-to-all-done.2.back_ref), custom_call_target="tpu_custom_call" | custom-call | tf_op jit(solution)/shard_map/combine_rows/pallas_call | solution.py:463
  (2 shorter events, 0.0 us)
Async XLA Ops:
  7.2 98.6 %all-to-all-start.1 = ((bf16[128,224,128]{2,1,0:T(8,128)(2,1)}), bf16[128,224,128]{2,1,0:T(8,128)(2,1)}, u32[]{:S(2)}, u32[]{:S(2)}) async-start(bf16[128,224,128]{2,1,0:T(8,128)(2,1)} %get-tuple-element.27), calls=%async_computation.1 | async-start | bytes 14680064 | tf_op jit(solution)/shard_map/all_to_all | solution.py:478
  19.2 95.0 %copy-start = (bf16[1,2048,768]{2,1,0:T(8,128)(2,1)S(1)}, bf16[1,2048,768]{2,1,0:T(8,128)(2,1)}, u32[]{:S(2)}) copy-start(bf16[1,2048,768]{2,1,0:T(8,128)(2,1)} %param.11) | copy-start | bytes 9437188
  105.9 38.3 %all-to-all-start = ((bf16[128,64,128]{2,1,0:T(8,128)(2,1)}), bf16[128,64,128]{2,1,0:T(8,128)(2,1)}, u32[]{:S(2)}, u32[]{:S(2)}) async-start(bf16[128,64,128]{2,1,0:T(8,128)(2,1)} %pack_rest.1), calls=%async_computation | async-start | bytes 4194304 | tf_op jit(solution)/shard_map/all_to_all | solution.py:478
  154.7 5.6 %copy-start.2 = (bf16[1152,768]{1,0:T(8,128)(2,1)S(1)}, bf16[1152,768]{1,0:T(8,128)(2,1)}, u32[]{:S(2)}) copy-start(bf16[1152,768]{1,0:T(8,128)(2,1)} %get-tuple-element.39) | copy-start | bytes 5308420
  154.7 13.9 %slice-start = ((s8[4718592]{0:T(1024)(128)(4,1)}), s8[524288]{0:T(1024)(128)(4,1)S(1)}, s32[]{:S(2)}) async-start(s8[4718592]{0:T(1024)(128)(4,1)} %bitcast.20), calls=%async_computation.3 | async-start | bytes 1048576
  154.7 66.7 %all-to-all-start.2 = ((bf16[128,152,128]{2,1,0:T(8,128)(2,1)}), bf16[128,152,128]{2,1,0:T(8,128)(2,1)}, u32[]{:S(2)}, u32[]{:S(2)}) async-start(bf16[128,152,128]{2,1,0:T(8,128)(2,1)} %get-tuple-element.35), calls=%async_computation.2 | async-start | bytes 9961472 | tf_op jit(solution)/shard_map/all_to_all | solution.py:478
  160.3 8.3 %slice-start.1 = ((s8[4718592]{0:T(1024)(128)(4,1)}), s8[4194304]{0:T(1024)(128)(4,1)S(1)}, s32[]{:S(2)}) async-start(s8[4718592]{0:T(1024)(128)(4,1)} %bitcast.20), calls=%async_computation.4 | async-start | bytes 8388608
  160.3 8.3 %copy-start.3 = (bf16[1152,768]{1,0:T(8,128)(2,1)S(1)}, bf16[1152,768]{1,0:T(8,128)(2,1)}, u32[]{:S(2)}) copy-start(bf16[1152,768]{1,0:T(8,128)(2,1)} %get-tuple-element.40) | copy-start | bytes 5308420
  160.3 14.0 %slice-start.2 = ((s8[4718592]{0:T(1024)(128)(4,1)}), s8[4194304]{0:T(1024)(128)(4,1)S(1)}, s32[]{:S(2)}) async-start(s8[4718592]{0:T(1024)(128)(4,1)} %bitcast.22), calls=%async_computation.5 | async-start | bytes 8388608
  168.6 5.7 %slice-start.3 = ((s8[4718592]{0:T(1024)(128)(4,1)}), s8[524288]{0:T(1024)(128)(4,1)S(1)}, s32[]{:S(2)}) async-start(s8[4718592]{0:T(1024)(128)(4,1)} %bitcast.22), calls=%async_computation.6 | async-start | bytes 1048576
  168.6 5.7 %copy-start.1 = (bf16[1152,768]{1,0:T(8,128)(2,1)S(1)}, bf16[1152,768]{1,0:T(8,128)(2,1)}, u32[]{:S(2)}) copy-start(bf16[1152,768]{1,0:T(8,128)(2,1)} %get-tuple-element.41) | copy-start | bytes 5308420

commit v3 on v2

--- a/solution.py
+++ b/solution.py
@@ -61,11 +61,18 @@
         for v in (token, gates)
     ]
     code = (expert_at * sub).astype(f32) + place
-    codes = [
-        jnp.sum(jnp.where(ids[k : k + 1, :] == expert_at, code, 0.0), axis=0, keepdims=True)
-        for k in range(top)
+    spot = (expert_at * (capacity * sub)).astype(f32) + place * float(sub)
+    codes, spots = [
+        jnp.concatenate(
+            [
+                jnp.sum(jnp.where(ids[k : k + 1, :] == expert_at, v, 0.0), axis=0, keepdims=True)
+                for k in range(top)
+            ],
+            axis=0,
+        ).astype(jnp.int32)
+        for v in (code, spot)
     ]
-    return index.astype(jnp.int32), scale, jnp.concatenate(codes, axis=0).astype(jnp.int32)
+    return index.astype(jnp.int32), scale, codes, spots
 
 
 def wide_to_tiles(swap, wide, chunks, store):
@@ -123,13 +130,14 @@
 
 def pack_first_kernel(
     start, count, ids_ref, num_ref, tok_ref, dy_ref,
-    out_hbm, index_ref, scale_ref, code_ref,
+    out_hbm, index_ref, scale_ref, code_ref, spot_ref,
     tok_tiles, dy_tiles, buffer, out_sems, index_s, scale_s, sems,
 ):
-    index, scale, code = spread_tables(ids_ref[...], num_ref[...], index_ref.shape[1])
+    index, scale, code, spot = spread_tables(ids_ref[...], num_ref[...], index_ref.shape[1])
     index_ref[...] = index
     scale_ref[...] = scale
     code_ref[...] = code
+    spot_ref[...] = spot
     one = pltpu.make_async_copy(index_ref, index_s, sems.at[0])
     two = pltpu.make_async_copy(scale_ref, scale_s, sems.at[1])
     one.start()
@@ -169,8 +177,9 @@
             jax.ShapeDtypeStruct((sub, experts), jnp.int32),
             jax.ShapeDtypeStruct((sub, experts), f32),
             jax.ShapeDtypeStruct(ids.shape, jnp.int32),
+            jax.ShapeDtypeStruct(ids.shape, jnp.int32),
         ]
-        out_specs += [vmem] * 3
+        out_specs += [vmem] * 4
         scratch += [
             pltpu.SMEM((sub, experts), jnp.int32),
             pltpu.SMEM((sub, experts), f32),
@@ -414,18 +423,18 @@
     )(*args)
 
 
-def combine_kernel(code_s_ref, code_ref, num_ref, back_ref, tok_ref, gate_ref, tiles_ref):
+def combine_kernel(spot_ref, code_ref, num_ref, back_ref, side_ref, tok_ref, gate_ref, tiles_ref):
     toks, width = tok_ref.shape
     top = code_ref.shape[0]
     chunks = width // lanes
     experts = back_ref.shape[0]
+    flat_ref = back_ref.reshape(experts * capacity * sub, lanes)
 
     def one(t, carry):
         total = None
         for k in range(top):
-            code = code_s_ref[k, t]
-            at = pl.multiple_of((code & 15) << 4, sub)
-            row = back_ref[code >> 4, pl.ds(at, sub), :].astype(f32)
+            at = pl.multiple_of(spot_ref[k, t], sub)
+            row = flat_ref[pl.ds(at, sub), :].astype(f32)
             total = row if total is None else total + row
         tiles_ref[t] = total.astype(bf16)
         return carry
@@ -443,7 +452,7 @@
                     j * sub : (j + 1) * sub, d * lanes : (d + 1) * lanes
                 ]
 
-    grads = jnp.max(back_ref[:, capacity * sub : capacity * sub + 8, :].astype(f32), axis=1)
+    grads = jnp.max(side_ref[...].astype(f32), axis=1)
     grads = jnp.transpose(grads).astype(bf16)
     gate = num_ref[...].astype(f32) * (1.0 / 256.0)
     expert_at = lax.broadcasted_iota(jnp.int32, (experts, toks), 0)
@@ -457,13 +466,26 @@
     gate_ref[...] = (jnp.concatenate(found, axis=0) / gate).astype(bf16)
 
 
-def combine(code, num, back, toks, width):
+def combine(spot, code, num, back, toks, width):
     top = code.shape[0]
-    vmem = pl.BlockSpec(memory_space=pltpu.VMEM)
+    experts = back.shape[0]
+
+    def rows_of(at, count):
+        return pl.BlockSpec(
+            (pl.Element(experts), pl.Element(count), pl.Element(lanes)), lambda i: (0, at, 0)
+        )
+
     return pl.pallas_call(
         combine_kernel,
-        in_specs=[pl.BlockSpec(memory_space=pltpu.SMEM), vmem, vmem, vmem],
-        out_specs=[vmem] * 2,
+        grid=(1,),
+        in_specs=[
+            pl.BlockSpec(memory_space=pltpu.SMEM),
+            whole(code.shape),
+            whole(num.shape),
+            rows_of(0, capacity * sub),
+            rows_of(capacity * sub, 8),
+        ],
+        out_specs=[whole((toks, width)), whole((top, toks))],
         out_shape=[
             jax.ShapeDtypeStruct((toks, width), bf16),
             jax.ShapeDtypeStruct((top, toks), bf16),
@@ -471,7 +493,7 @@
         scratch_shapes=[pltpu.VMEM((toks, width // lanes, lanes), bf16)],
         compiler_params=params(60),
         name="combine_rows",
-    )(code, code, num, back)
+    )(spot, code, num, back, back)
 
 
 def exchange(rows):
@@ -484,7 +506,7 @@
     wg, wu, wd = w_gate[0], w_up[0], w_down[0]
     ids, num = expert_ids.T, gate_num.T
     rest = capacity - first_rows
-    first, index, scale, code = pack(tokens, d_out, 0, first_rows, experts, ids, num)
+    first, index, scale, code, spot = pack(tokens, d_out, 0, first_rows, experts, ids, num)
     (second,) = pack(tokens, d_out, first_rows, rest, experts, tables=(index, scale))
     first, second = exchange(first), exchange(second)
     part = expert_rows(first, wg, wu, wd, 0, first_rows, 64)
@@ -493,7 +515,7 @@
     grad_gate = lax.dot_general(rows_x, da, contract_rows, preferred_element_type=f32).astype(bf16)
     grad_up = lax.dot_general(rows_x, db, contract_rows, preferred_element_type=f32).astype(bf16)
     grad_down = lax.dot_general(h, rows_dy, contract_rows, preferred_element_type=f32).astype(bf16)
-    d_tokens, d_gate = combine(code, num, back, toks, width)
+    d_tokens, d_gate = combine(spot, code, num, back, toks, width)
     return (d_tokens, d_gate.T, grad_gate[None], grad_up[None], grad_down[None])
 
 

time: 229 us -> 227 us (level)
  no operation moved by 1% of the time
where the time goes in v3:
time: 227 us
  waiting for transfers between devices  130 us (57%)
  Pallas kernels  50.4 us (22%)
  starting transfers between devices  25.8 us (11%)
  matrix products  19.6 us (9%)
    all_to_all x3, waiting for transfers between devices, exchange(): lax.all_to_all(rows, ('dp', 'expert'), split_axis=0, concat_axis=0, tiled...  130 us
    pallas_call x2, Pallas kernels, expert_rows(): pl.pallas_call(functools.partial(expert_kernel, start, count, block, last...  34.6 us
    all_to_all x3, starting transfers between devices, exchange(): lax.all_to_all(rows, ('dp', 'expert'), split_axis=0, concat_axis=0, tiled...  25.8 us
    pallas_call x2, Pallas kernels, pack(): pl.pallas_call(body, in_specs=in_specs, out_specs=out_specs, out_shape=ou...  10.3 us
    dot_general x1, matrix products, local(): lax.dot_general(rows_x, da, contract_rows, preferred_element_type=f32)  8.27 us
    dot_general x1, matrix products, local(): lax.dot_general(rows_x, db, contract_rows, preferred_element_type=f32)  5.72 us
    dot_general x1, matrix products, local(): lax.dot_general(h, rows_dy, contract_rows, preferred_element_type=f32)  5.64 us
    pallas_call x1, Pallas kernels, combine(): pl.pallas_call(combine_kernel, grid=(1,), in_specs=[pl.BlockSpec(memory_s...  5.42 us
  transfers between devices with their start and end apart: 3, of which 3 were waited for; matrix products, arithmetic and copies ran while one was open for 9% of the time, Pallas kernels for 12%

profile of v3, /device:TPU:1, one launch (start us, length us, event | category | flops | bytes accessed | tf_op | source)
XLA Modules:
  0.0 226.9 jit_solution(2844580298152618067)
XLA Ops:
  0.6 6.7 %pack_first.1 = (bf16[128,224,128]{2,1,0:T(8,128)(2,1)}, s32[16,128]{1,0:T(8,128)}, f32[16,128]{1,0:T(8,128)}, s32[8,128]{1,0:T(8,128)}, s32[8,128]{1,0:T(8,128)}) custom-call(s32[8,128]{1,0:T(8,128)} %bitcast.30, s32[8,128]{1,0:T(8,128)} %bitcast.28, bf16[128,2048]{1,0:T(8,128)(2,1)} %tok_ref.3, bf16[128,2048]{1,0:T(8,128)(2,1)} %dy_ref.3), custom_call_target="tpu_custom_call" | custom-call | bytes 7340032 | tf_op jit(solution)/shard_map/pack_first/pallas_call | solution.py:192
  7.3 11.9 %all-to-all-start.1 = ((bf16[128,224,128]{2,1,0:T(8,128)(2,1)}), bf16[128,224,128]{2,1,0:T(8,128)(2,1)}, u32[]{:S(2)}, u32[]{:S(2)}) async-start(bf16[128,224,128]{2,1,0:T(8,128)(2,1)} %get-tuple-element.29), calls=%async_computation.1 | async-start | bytes 14680064 | tf_op jit(solution)/shard_map/all_to_all | solution.py:500
  19.2 0.0 copy-start
  19.2 3.7 %pack_rest.1 = bf16[128,64,128]{2,1,0:T(8,128)(2,1)} custom-call(s32[16,128]{1,0:T(8,128)} %get-tuple-element.27.index_ref, f32[16,128]{1,0:T(8,128)} %get-tuple-element.28.scale_ref, bf16[128,2048]{1,0:T(8,128)(2,1)} %tok_ref.3, bf16[128,2048]{1,0:T(8,128)(2,1)} %dy_ref.3), custom_call_target="tpu_custom_call" | custom-call | bytes 2097152 | tf_op jit(solution)/shard_map/pack_rest/pallas_call | solution.py:192
  22.9 83.0 %all-to-all-done.1.refs_0_ = bf16[128,224,128]{2,1,0:T(8,128)(2,1)} async-done(((bf16[128,224,128]{2,1,0:T(8,128)(2,1)}), bf16[128,224,128]{2,1,0:T(8,128)(2,1)}, u32[]{:S(2)}, u32[]{:S(2)}) %all-to-all-start.1) | async-done | bytes 7340064 | tf_op jit(solution)/shard_map/all_to_all | solution.py:500
  105.9 8.3 %all-to-all-start = ((bf16[128,64,128]{2,1,0:T(8,128)(2,1)}), bf16[128,64,128]{2,1,0:T(8,128)(2,1)}, u32[]{:S(2)}, u32[]{:S(2)}) async-start(bf16[128,64,128]{2,1,0:T(8,128)(2,1)} %pack_rest.1), calls=%async_computation | async-start | bytes 4194304 | tf_op jit(solution)/shard_map/all_to_all | solution.py:500
  114.2 0.0 copy-done
  114.3 24.2 %expert_rows_first.1 = (bf16[1152,2048]{1,0:T(8,128)(2,1)}, bf16[1152,2048]{1,0:T(8,128)(2,1)}, bf16[1152,768]{1,0:T(8,128)(2,1)}, bf16[1152,768]{1,0:T(8,128)(2...) custom-call(bf16[128,224,128]{2,1,0:T(8,128)(2,1)} %all-to-all-done.1.refs_0_, ...), custom_call_target="tpu_custom_call" | custom-call | flops 14092861440 | bytes 31457280 | tf_op jit(solution)/shard_map/expert_rows_first/pallas_call | solution.py:394
  138.4 5.8 %all-to-all-done.refs_0_ = bf16[128,64,128]{2,1,0:T(8,128)(2,1)} async-done(((bf16[128,64,128]{2,1,0:T(8,128)(2,1)}), bf16[128,64,128]{2,1,0:T(8,128)(2,1)}, u32[]{:S(2)}, u32[]{:S(2)}) %all-to-all-start) | async-done | bytes 2097184 | tf_op jit(solution)/shard_map/all_to_all | solution.py:500
  144.2 10.5 %expert_rows_last.1 = (bf16[1152,2048]{1,0:T(8,128)(2,1)}, bf16[1152,2048]{1,0:T(8,128)(2,1)}, bf16[1152,768]{1,0:T(8,128)(2,1)}, bf16[1152,768]{1,0:T(8,128)(2,...) custom-call(bf16[128,64,128]{2,1,0:T(8,128)(2,1)} %all-to-all-done.r, ...), custom_call_target="tpu_custom_call", output_to_operand_aliasing={{0}: (5, {}), {1}: (6, {}), {2}: (7, {}), {3}: (8, {}), {4}... | custom-call | flops 4026531840 | bytes 15728640 | tf_op jit(solution)/shard_map/expert_rows_last/pallas_call | solution.py:394
  154.7 0.0 copy-start.2
  154.7 0.0 slice-start
  154.7 5.6 %all-to-all-start.2 = ((bf16[128,152,128]{2,1,0:T(8,128)(2,1)}), bf16[128,152,128]{2,1,0:T(8,128)(2,1)}, u32[]{:S(2)}, u32[]{:S(2)}) async-start(bf16[128,152,128]{2,1,0:T(8,128)(2,1)} %get-tuple-element.37), calls=%async_computation.2 | async-start | bytes 9961472 | tf_op jit(solution)/shard_map/all_to_all | solution.py:500
  160.3 0.0 copy-done.2
  160.3 0.0 slice-start.1
  160.4 0.0 copy-start.3
  160.4 0.0 slice-start.2
  160.4 8.3 %fusion = bf16[1,2048,768]{2,1,0:T(8,128)(2,1)} fusion(bf16[1152,2048]{1,0:T(8,128)(2,1)} %get-tuple-element.40, bf16[1152,768]{1,0:T(8,128)(2,1)S(1)} %copy-done.2), kind=kOutput, calls=%fused_computation.3 | convolution fusion | flops 3625451520 | bytes 9633792 | tf_op jit(solution)/shard_map/dot_general | solution.py:515
  168.6 0.0 slice-done
  168.6 0.0 slice-done.1
  168.6 0.0 copy-done.3
  168.7 0.0 slice-start.3
  168.7 0.0 copy-start.1
  168.7 5.7 %fusion.1 = bf16[1,2048,768]{2,1,0:T(8,128)(2,1)} fusion(bf16[1152,2048]{1,0:T(8,128)(2,1)S(1)} %bitcast.21, bf16[1152,768]{1,0:T(8,128)(2,1)S(1)} %copy-done.3), kind=kOutput, calls=%fused_computation.4 | convolution fusion | flops 3625451520 | bytes 9633792 | tf_op jit(solution)/shard_map/dot_general | solution.py:516
  174.4 0.0 slice-done.2
  174.4 0.0 slice-done.3
  174.4 0.0 copy-done.1
  174.4 5.6 %fusion.2 = bf16[1,768,2048]{2,1,0:T(8,128)(2,1)} fusion(bf16[1152,768]{1,0:T(8,128)(2,1)S(1)} %copy-done.1, bf16[1152,2048]{1,0:T(8,128)(2,1)S(1)} %bitcast.23), kind=kOutput, calls=%fused_computation.5 | convolution fusion | flops 3625451520 | bytes 9633792 | tf_op jit(solution)/shard_map/dot_general | solution.py:517
  180.1 41.4 %all-to-all-done.2.back_ref.side_ref = bf16[128,152,128]{2,1,0:T(8,128)(2,1)} async-done(((bf16[128,152,128]{2,1,0:T(8,128)(2,1)}), bf16[128,152,128]{2,1,0:T(8,128)(2,1)}, u32[]{:S(2)}, u32[]{:S(2)}) %all-to-all-start.2) | async-done | bytes 4980768 | tf_op jit(solution)/shard_map/all_to_all | solution.py:500
  221.4 5.4 %combine_rows.1 = (bf16[128,2048]{1,0:T(8,128)(2,1)}, bf16[8,128]{1,0:T(8,128)(2,1)}) custom-call(s32[8,128]{1,0:T(8,128)} %get-tuple-element.25.spot_ref, s32[8,128]{1,0:T(8,128)} %get-tuple-element.26.code_ref, s32[8,128]{1,0:T(8,128)} %bitcast.29, bf16[128,152,128]{2,1,0:T(8,128)(2,1)} %all-to-all-done.2.back_ref.side_ref, ...), custom_call_target="tpu_custom_call" | custom-call | tf_op jit(solution)/shard_map/combine_rows/pallas_call | solution.py:478
  (2 shorter events, 0.0 us)
Async XLA Ops:
  7.3 98.6 %all-to-all-start.1 = ((bf16[128,224,128]{2,1,0:T(8,128)(2,1)}), bf16[128,224,128]{2,1,0:T(8,128)(2,1)}, u32[]{:S(2)}, u32[]{:S(2)}) async-start(bf16[128,224,128]{2,1,0:T(8,128)(2,1)} %get-tuple-element.29), calls=%async_computation.1 | async-start | bytes 14680064 | tf_op jit(solution)/shard_map/all_to_all | solution.py:500
  19.2 95.0 %copy-start = (bf16[1,2048,768]{2,1,0:T(8,128)(2,1)S(1)}, bf16[1,2048,768]{2,1,0:T(8,128)(2,1)}, u32[]{:S(2)}) copy-start(bf16[1,2048,768]{2,1,0:T(8,128)(2,1)} %param.11) | copy-start | bytes 9437188
  105.9 38.3 %all-to-all-start = ((bf16[128,64,128]{2,1,0:T(8,128)(2,1)}), bf16[128,64,128]{2,1,0:T(8,128)(2,1)}, u32[]{:S(2)}, u32[]{:S(2)}) async-start(bf16[128,64,128]{2,1,0:T(8,128)(2,1)} %pack_rest.1), calls=%async_computation | async-start | bytes 4194304 | tf_op jit(solution)/shard_map/all_to_all | solution.py:500
  154.7 5.6 %copy-start.2 = (bf16[1152,768]{1,0:T(8,128)(2,1)S(1)}, bf16[1152,768]{1,0:T(8,128)(2,1)}, u32[]{:S(2)}) copy-start(bf16[1152,768]{1,0:T(8,128)(2,1)} %get-tuple-element.41) | copy-start | bytes 5308420
  154.7 13.9 %slice-start = ((s8[4718592]{0:T(1024)(128)(4,1)}), s8[524288]{0:T(1024)(128)(4,1)S(1)}, s32[]{:S(2)}) async-start(s8[4718592]{0:T(1024)(128)(4,1)} %bitcast.20), calls=%async_computation.3 | async-start | bytes 1048576
  154.7 66.7 %all-to-all-start.2 = ((bf16[128,152,128]{2,1,0:T(8,128)(2,1)}), bf16[128,152,128]{2,1,0:T(8,128)(2,1)}, u32[]{:S(2)}, u32[]{:S(2)}) async-start(bf16[128,152,128]{2,1,0:T(8,128)(2,1)} %get-tuple-element.37), calls=%async_computation.2 | async-start | bytes 9961472 | tf_op jit(solution)/shard_map/all_to_all | solution.py:500
  160.3 8.3 %slice-start.1 = ((s8[4718592]{0:T(1024)(128)(4,1)}), s8[4194304]{0:T(1024)(128)(4,1)S(1)}, s32[]{:S(2)}) async-start(s8[4718592]{0:T(1024)(128)(4,1)} %bitcast.20), calls=%async_computation.4 | async-start | bytes 8388608
  160.4 8.3 %copy-start.3 = (bf16[1152,768]{1,0:T(8,128)(2,1)S(1)}, bf16[1152,768]{1,0:T(8,128)(2,1)}, u32[]{:S(2)}) copy-start(bf16[1152,768]{1,0:T(8,128)(2,1)} %get-tuple-element.42) | copy-start | bytes 5308420
  160.4 14.0 %slice-start.2 = ((s8[4718592]{0:T(1024)(128)(4,1)}), s8[4194304]{0:T(1024)(128)(4,1)S(1)}, s32[]{:S(2)}) async-start(s8[4718592]{0:T(1024)(128)(4,1)} %bitcast.22), calls=%async_computation.5 | async-start | bytes 8388608
  168.7 5.7 %slice-start.3 = ((s8[4718592]{0:T(1024)(128)(4,1)}), s8[524288]{0:T(1024)(128)(4,1)S(1)}, s32[]{:S(2)}) async-start(s8[4718592]{0:T(1024)(128)(4,1)} %bitcast.22), calls=%async_computation.6 | async-start | bytes 1048576
  168.7 5.7 %copy-start.1 = (bf16[1152,768]{1,0:T(8,128)(2,1)S(1)}, bf16[1152,768]{1,0:T(8,128)(2,1)}, u32[]{:S(2)}) copy-start(bf16[1152,768]{1,0:T(8,128)(2,1)} %get-tuple-element.43) | copy-start | bytes 5308420

commit v4 on v3

--- a/solution.py
+++ b/solution.py
@@ -129,19 +129,25 @@
 
 
 def pack_first_kernel(
-    start, count, ids_ref, num_ref, tok_ref, dy_ref,
+    start, count, ids_ref, num_ref, tok_hbm, dy_hbm,
     out_hbm, index_ref, scale_ref, code_ref, spot_ref,
-    tok_tiles, dy_tiles, buffer, out_sems, index_s, scale_s, sems,
+    tok_tiles, dy_tiles, buffer, out_sems, index_s, scale_s, tok_ref, dy_ref, sems,
 ):
+    tok_in = pltpu.make_async_copy(tok_hbm, tok_ref, sems.at[2])
+    dy_in = pltpu.make_async_copy(dy_hbm, dy_ref, sems.at[3])
+    tok_in.start()
+    dy_in.start()
     index, scale, code, spot = spread_tables(ids_ref[...], num_ref[...], index_ref.shape[1])
     index_ref[...] = index
     scale_ref[...] = scale
-    code_ref[...] = code
-    spot_ref[...] = spot
     one = pltpu.make_async_copy(index_ref, index_s, sems.at[0])
     two = pltpu.make_async_copy(scale_ref, scale_s, sems.at[1])
     one.start()
     two.start()
+    code_ref[...] = code
+    spot_ref[...] = spot
+    tok_in.wait()
+    dy_in.wait()
     make_tiles(tok_ref, dy_ref, tok_tiles, dy_tiles)
     one.wait()
     two.wait()
@@ -172,7 +178,7 @@
     if tables is None:
         body = functools.partial(pack_first_kernel, start, count)
         args = (ids, num, tokens, d_out)
-        in_specs = [vmem] * 4
+        in_specs = [vmem] * 2 + [pl.BlockSpec(memory_space=pl.ANY)] * 2
         out_shape += [
             jax.ShapeDtypeStruct((sub, experts), jnp.int32),
             jax.ShapeDtypeStruct((sub, experts), f32),
@@ -183,7 +189,9 @@
         scratch += [
             pltpu.SMEM((sub, experts), jnp.int32),
             pltpu.SMEM((sub, experts), f32),
-            pltpu.SemaphoreType.DMA((2,)),
+            pltpu.VMEM(tokens.shape, bf16),
+            pltpu.VMEM(d_out.shape, bf16),
+            pltpu.SemaphoreType.DMA((4,)),
         ]
     else:
         body = functools.partial(pack_rest_kernel, start, count)
@@ -207,7 +215,7 @@
     (wire_hbm, wg, wu_hbm, wd_hbm) = refs[:4]
     refs = refs[4:]
     if last:
-        old_gate_ref = refs[0]
+        old_gate_hbm = refs[0]
         refs = refs[7:]
     out_hbm = refs[:5]
     back_ref = refs[5]
@@ -216,7 +224,10 @@
         gate_ref = refs[0]
         refs = refs[1:]
     (wire, wu, wd, x_ref, dy_ref, h_ref, da_ref, db_ref, dx_ref, swap_ref) = refs[:10]
-    (wire_sem, weight_sem, out_sem) = refs[10:]
+    (wire_sem, weight_sem, out_sem) = refs[10:13]
+    if last:
+        (old_gate_ref, old_gate_sem) = refs[13:]
+        old_gate = pltpu.make_async_copy(old_gate_hbm, old_gate_ref, old_gate_sem)
     sources = wire_hbm.shape[0]
     blocks = sources // block
     rows = block * count
@@ -248,6 +259,8 @@
     for b in range(1, blocks):
         wire_copy(b, 0).start()
         wire_copy(b, 1).start()
+    if last:
+        old_gate.start()
     swap_ref[...] = swap_matrix()
 
     def widen(b, side, out):
@@ -310,6 +323,8 @@
 
         lane = lax.broadcasted_iota(jnp.int32, (block, lanes), 1)
         at = slice(b * block, (b + 1) * block)
+        if last:
+            old_gate.wait()
         gates = old_gate_ref[at, :] if last else jnp.zeros((block, lanes), f32)
         for p in range(count):
             gates = jnp.where(lane == start + p, gate_grad[p * block : (p + 1) * block], gates)
@@ -385,12 +400,15 @@
     args = [wire, pltpu.with_memory_space_constraint(wg, pltpu.VMEM), wu, wd]
     aliases = {}
     if last:
-        in_specs += [whole((sources, lanes))] + [anywhere] * 6
+        in_specs += [anywhere] * 7
         args += [carry[6]] + list(carry[:6])
         aliases = {5 + i: i for i in range(6)}
     else:
         out_specs.append(whole((sources, lanes)))
         out_shape.append(jax.ShapeDtypeStruct((sources, lanes), f32))
+    scratch = []
+    if last:
+        scratch = [pltpu.VMEM((sources, lanes), f32), pltpu.SemaphoreType.DMA]
     return pl.pallas_call(
         functools.partial(expert_kernel, start, count, block, last),
         grid=(1,),
@@ -411,7 +429,8 @@
             pltpu.SemaphoreType.DMA((sources // block, 2)),
             pltpu.SemaphoreType.DMA((2,)),
             pltpu.SemaphoreType.DMA((5, sources // block)),
-        ],
+        ]
+        + scratch,
         input_output_aliases=aliases,
         compiler_params=params(60),
         cost_estimate=pl.CostEstimate(

time: 227 us -> 226 us (level)
  no operation moved by 1% of the time
where the time goes in v4:
time: 226 us
  waiting for transfers between devices  130 us (58%)
  Pallas kernels  49.6 us (22%)
  starting transfers between devices  25.8 us (11%)
  matrix products  19.6 us (9%)
    all_to_all x3, waiting for transfers between devices, exchange(): lax.all_to_all(rows, ('dp', 'expert'), split_axis=0, concat_axis=0, tiled...  130 us
    pallas_call x2, Pallas kernels, expert_rows(): pl.pallas_call(functools.partial(expert_kernel, start, count, block, last...  34.1 us
    all_to_all x3, starting transfers between devices, exchange(): lax.all_to_all(rows, ('dp', 'expert'), split_axis=0, concat_axis=0, tiled...  25.8 us
    pallas_call x2, Pallas kernels, pack(): pl.pallas_call(body, in_specs=in_specs, out_specs=out_specs, out_shape=ou...  10.1 us
    dot_general x1, matrix products, local(): lax.dot_general(rows_x, da, contract_rows, preferred_element_type=f32)  8.26 us
    dot_general x1, matrix products, local(): lax.dot_general(rows_x, db, contract_rows, preferred_element_type=f32)  5.74 us
    dot_general x1, matrix products, local(): lax.dot_general(h, rows_dy, contract_rows, preferred_element_type=f32)  5.64 us
    pallas_call x1, Pallas kernels, combine(): pl.pallas_call(combine_kernel, grid=(1,), in_specs=[pl.BlockSpec(memory_s...  5.42 us
  transfers between devices with their start and end apart: 3, of which 3 were waited for; matrix products, arithmetic and copies ran while one was open for 9% of the time, Pallas kernels for 12%

profile of v4, /device:TPU:1, one launch (start us, length us, event | category | flops | bytes accessed | tf_op | source)
XLA Modules:
  0.0 226.1 jit_solution(11239574113013061369)
XLA Ops:
  0.6 6.4 %pack_first.1 = (bf16[128,224,128]{2,1,0:T(8,128)(2,1)}, s32[16,128]{1,0:T(8,128)}, f32[16,128]{1,0:T(8,128)}, s32[8,128]{1,0:T(8,128)}, s32[8,128]{1,0:T(8,128)}) custom-call(s32[8,128]{1,0:T(8,128)} %bitcast.30, s32[8,128]{1,0:T(8,128)} %bitcast.28, bf16[128,2048]{1,0:T(8,128)(2,1)} %tok_ref.1, bf16[128,2048]{1,0:T(8,128)(2,1)} %dy_ref.1), custom_call_target="tpu_custom_call" | custom-call | bytes 7340032 | tf_op jit(solution)/shard_map/pack_first/pallas_call | solution.py:200
  7.1 11.9 %all-to-all-start.1 = ((bf16[128,224,128]{2,1,0:T(8,128)(2,1)}), bf16[128,224,128]{2,1,0:T(8,128)(2,1)}, u32[]{:S(2)}, u32[]{:S(2)}) async-start(bf16[128,224,128]{2,1,0:T(8,128)(2,1)} %get-tuple-element.29), calls=%async_computation.1 | async-start | bytes 14680064 | tf_op jit(solution)/shard_map/all_to_all | solution.py:519
  19.0 0.0 copy-start
  19.0 3.6 %pack_rest.1 = bf16[128,64,128]{2,1,0:T(8,128)(2,1)} custom-call(s32[16,128]{1,0:T(8,128)} %get-tuple-element.27.index_ref, f32[16,128]{1,0:T(8,128)} %get-tuple-element.28.scale_ref, bf16[128,2048]{1,0:T(8,128)(2,1)} %tok_ref.1, bf16[128,2048]{1,0:T(8,128)(2,1)} %dy_ref.1), custom_call_target="tpu_custom_call" | custom-call | bytes 2097152 | tf_op jit(solution)/shard_map/pack_rest/pallas_call | solution.py:200
  22.7 83.0 %all-to-all-done.1.refs_0_ = bf16[128,224,128]{2,1,0:T(8,128)(2,1)} async-done(((bf16[128,224,128]{2,1,0:T(8,128)(2,1)}), bf16[128,224,128]{2,1,0:T(8,128)(2,1)}, u32[]{:S(2)}, u32[]{:S(2)}) %all-to-all-start.1) | async-done | bytes 7340064 | tf_op jit(solution)/shard_map/all_to_all | solution.py:519
  105.7 8.3 %all-to-all-start = ((bf16[128,64,128]{2,1,0:T(8,128)(2,1)}), bf16[128,64,128]{2,1,0:T(8,128)(2,1)}, u32[]{:S(2)}, u32[]{:S(2)}) async-start(bf16[128,64,128]{2,1,0:T(8,128)(2,1)} %pack_rest.1), calls=%async_computation | async-start | bytes 4194304 | tf_op jit(solution)/shard_map/all_to_all | solution.py:519
  114.0 0.0 copy-done
  114.0 24.2 %expert_rows_first.1 = (bf16[1152,2048]{1,0:T(8,128)(2,1)}, bf16[1152,2048]{1,0:T(8,128)(2,1)}, bf16[1152,768]{1,0:T(8,128)(2,1)}, bf16[1152,768]{1,0:T(8,128)(2...) custom-call(bf16[128,224,128]{2,1,0:T(8,128)(2,1)} %all-to-all-done.1.refs_0_, ...), custom_call_target="tpu_custom_call" | custom-call | flops 14092861440 | bytes 31457280 | tf_op jit(solution)/shard_map/expert_rows_first/pallas_call | solution.py:412
  138.2 5.8 %all-to-all-done.refs_0_ = bf16[128,64,128]{2,1,0:T(8,128)(2,1)} async-done(((bf16[128,64,128]{2,1,0:T(8,128)(2,1)}), bf16[128,64,128]{2,1,0:T(8,128)(2,1)}, u32[]{:S(2)}, u32[]{:S(2)}) %all-to-all-start) | async-done | bytes 2097184 | tf_op jit(solution)/shard_map/all_to_all | solution.py:519
  144.0 9.9 %expert_rows_last.1 = (bf16[1152,2048]{1,0:T(8,128)(2,1)}, bf16[1152,2048]{1,0:T(8,128)(2,1)}, bf16[1152,768]{1,0:T(8,128)(2,1)}, bf16[1152,768]{1,0:T(8,128)(2,...) custom-call(bf16[128,64,128]{2,1,0:T(8,128)(2,1)} %all-to-all-done.r, ...), custom_call_target="tpu_custom_call", output_to_operand_aliasing={{0}: (5, {}), {1}: (6, {}), {2}: (7, {}), {3}: (8, {}), {4}... | custom-call | flops 4026531840 | bytes 15728640 | tf_op jit(solution)/shard_map/expert_rows_last/pallas_call | solution.py:412
  153.9 0.0 copy-start.2
  153.9 0.0 slice-start
  153.9 5.6 %all-to-all-start.2 = ((bf16[128,152,128]{2,1,0:T(8,128)(2,1)}), bf16[128,152,128]{2,1,0:T(8,128)(2,1)}, u32[]{:S(2)}, u32[]{:S(2)}) async-start(bf16[128,152,128]{2,1,0:T(8,128)(2,1)} %get-tuple-element.37), calls=%async_computation.2 | async-start | bytes 9961472 | tf_op jit(solution)/shard_map/all_to_all | solution.py:519
  159.6 0.0 copy-done.2
  159.6 0.0 slice-start.1
  159.6 0.0 copy-start.3
  159.6 0.0 slice-start.2
  159.6 8.3 %fusion = bf16[1,2048,768]{2,1,0:T(8,128)(2,1)} fusion(bf16[1152,2048]{1,0:T(8,128)(2,1)} %get-tuple-element.40, bf16[1152,768]{1,0:T(8,128)(2,1)S(1)} %copy-done.2), kind=kOutput, calls=%fused_computation.3 | convolution fusion | flops 3625451520 | bytes 9633792 | tf_op jit(solution)/shard_map/dot_general | solution.py:534
  167.9 0.0 slice-done
  167.9 0.0 slice-done.1
  167.9 0.0 copy-done.3
  167.9 0.0 slice-start.3
  167.9 0.0 copy-start.1
  167.9 5.7 %fusion.1 = bf16[1,2048,768]{2,1,0:T(8,128)(2,1)} fusion(bf16[1152,2048]{1,0:T(8,128)(2,1)S(1)} %bitcast.21, bf16[1152,768]{1,0:T(8,128)(2,1)S(1)} %copy-done.3), kind=kOutput, calls=%fused_computation.4 | convolution fusion | flops 3625451520 | bytes 9633792 | tf_op jit(solution)/shard_map/dot_general | solution.py:535
  173.6 0.0 slice-done.2
  173.7 0.0 slice-done.3
  173.7 0.0 copy-done.1
  173.7 5.6 %fusion.2 = bf16[1,768,2048]{2,1,0:T(8,128)(2,1)} fusion(bf16[1152,768]{1,0:T(8,128)(2,1)S(1)} %copy-done.1, bf16[1152,2048]{1,0:T(8,128)(2,1)S(1)} %bitcast.23), kind=kOutput, calls=%fused_computation.5 | convolution fusion | flops 3625451520 | bytes 9633792 | tf_op jit(solution)/shard_map/dot_general | solution.py:536
  179.3 41.4 %all-to-all-done.2.back_ref.side_ref = bf16[128,152,128]{2,1,0:T(8,128)(2,1)} async-done(((bf16[128,152,128]{2,1,0:T(8,128)(2,1)}), bf16[128,152,128]{2,1,0:T(8,128)(2,1)}, u32[]{:S(2)}, u32[]{:S(2)}) %all-to-all-start.2) | async-done | bytes 4980768 | tf_op jit(solution)/shard_map/all_to_all | solution.py:519
  220.7 5.4 %combine_rows.1 = (bf16[128,2048]{1,0:T(8,128)(2,1)}, bf16[8,128]{1,0:T(8,128)(2,1)}) custom-call(s32[8,128]{1,0:T(8,128)} %get-tuple-element.25.spot_ref, s32[8,128]{1,0:T(8,128)} %get-tuple-element.26.code_ref, s32[8,128]{1,0:T(8,128)} %bitcast.29, bf16[128,152,128]{2,1,0:T(8,128)(2,1)} %all-to-all-done.2.back_ref.side_ref, ...), custom_call_target="tpu_custom_call" | custom-call | tf_op jit(solution)/shard_map/combine_rows/pallas_call | solution.py:497
  (2 shorter events, 0.0 us)
Async XLA Ops:
  7.1 98.6 %all-to-all-start.1 = ((bf16[128,224,128]{2,1,0:T(8,128)(2,1)}), bf16[128,224,128]{2,1,0:T(8,128)(2,1)}, u32[]{:S(2)}, u32[]{:S(2)}) async-start(bf16[128,224,128]{2,1,0:T(8,128)(2,1)} %get-tuple-element.29), calls=%async_computation.1 | async-start | bytes 14680064 | tf_op jit(solution)/shard_map/all_to_all | solution.py:519
  19.0 95.0 %copy-start = (bf16[1,2048,768]{2,1,0:T(8,128)(2,1)S(1)}, bf16[1,2048,768]{2,1,0:T(8,128)(2,1)}, u32[]{:S(2)}) copy-start(bf16[1,2048,768]{2,1,0:T(8,128)(2,1)} %param.11) | copy-start | bytes 9437188
  105.7 38.3 %all-to-all-start = ((bf16[128,64,128]{2,1,0:T(8,128)(2,1)}), bf16[128,64,128]{2,1,0:T(8,128)(2,1)}, u32[]{:S(2)}, u32[]{:S(2)}) async-start(bf16[128,64,128]{2,1,0:T(8,128)(2,1)} %pack_rest.1), calls=%async_computation | async-start | bytes 4194304 | tf_op jit(solution)/shard_map/all_to_all | solution.py:519
  153.9 5.6 %copy-start.2 = (bf16[1152,768]{1,0:T(8,128)(2,1)S(1)}, bf16[1152,768]{1,0:T(8,128)(2,1)}, u32[]{:S(2)}) copy-start(bf16[1152,768]{1,0:T(8,128)(2,1)} %get-tuple-element.41) | copy-start | bytes 5308420
  153.9 13.9 %slice-start = ((s8[4718592]{0:T(1024)(128)(4,1)}), s8[524288]{0:T(1024)(128)(4,1)S(1)}, s32[]{:S(2)}) async-start(s8[4718592]{0:T(1024)(128)(4,1)} %bitcast.20), calls=%async_computation.3 | async-start | bytes 1048576
  153.9 66.7 %all-to-all-start.2 = ((bf16[128,152,128]{2,1,0:T(8,128)(2,1)}), bf16[128,152,128]{2,1,0:T(8,128)(2,1)}, u32[]{:S(2)}, u32[]{:S(2)}) async-start(bf16[128,152,128]{2,1,0:T(8,128)(2,1)} %get-tuple-element.37), calls=%async_computation.2 | async-start | bytes 9961472 | tf_op jit(solution)/shard_map/all_to_all | solution.py:519
  159.6 8.3 %slice-start.1 = ((s8[4718592]{0:T(1024)(128)(4,1)}), s8[4194304]{0:T(1024)(128)(4,1)S(1)}, s32[]{:S(2)}) async-start(s8[4718592]{0:T(1024)(128)(4,1)} %bitcast.20), calls=%async_computation.4 | async-start | bytes 8388608
  159.6 8.3 %copy-start.3 = (bf16[1152,768]{1,0:T(8,128)(2,1)S(1)}, bf16[1152,768]{1,0:T(8,128)(2,1)}, u32[]{:S(2)}) copy-start(bf16[1152,768]{1,0:T(8,128)(2,1)} %get-tuple-element.42) | copy-start | bytes 5308420
  159.6 14.1 %slice-start.2 = ((s8[4718592]{0:T(1024)(128)(4,1)}), s8[4194304]{0:T(1024)(128)(4,1)S(1)}, s32[]{:S(2)}) async-start(s8[4718592]{0:T(1024)(128)(4,1)} %bitcast.22), calls=%async_computation.5 | async-start | bytes 8388608
  167.9 5.8 %slice-start.3 = ((s8[4718592]{0:T(1024)(128)(4,1)}), s8[524288]{0:T(1024)(128)(4,1)S(1)}, s32[]{:S(2)}) async-start(s8[4718592]{0:T(1024)(128)(4,1)} %bitcast.22), calls=%async_computation.6 | async-start | bytes 1048576
  167.9 5.8 %copy-start.1 = (bf16[1152,768]{1,0:T(8,128)(2,1)S(1)}, bf16[1152,768]{1,0:T(8,128)(2,1)}, u32[]{:S(2)}) copy-start(bf16[1152,768]{1,0:T(8,128)(2,1)} %get-tuple-element.43) | copy-start | bytes 5308420

commit v5 on v4

--- a/solution.py
+++ b/solution.py
@@ -172,7 +172,7 @@
         pltpu.VMEM((toks, chunks, lanes), bf16),
         pltpu.VMEM((toks, chunks, lanes), f32),
         pltpu.VMEM(wire, bf16),
-        pltpu.SemaphoreType.DMA((8,)),
+        pltpu.SemaphoreType.DMA((16,)),
     ]
     vmem = pl.BlockSpec(memory_space=pltpu.VMEM)
     if tables is None:
@@ -236,9 +236,16 @@
     part = 256
     half = count * sub
 
-    def wire_copy(b, side):
-        at = (slice(b * block, (b + 1) * block), slice(side * half, (side + 1) * half))
-        return pltpu.make_async_copy(wire_hbm.at[at], wire.at[at], wire_sem.at[b, side])
+    near = block // 2
+
+    def wire_copy(b, side, piece):
+        low = b * block + piece * near
+        at = (slice(low, low + near), slice(side * half, (side + 1) * half))
+        return pltpu.make_async_copy(wire_hbm.at[at], wire.at[at], wire_sem.at[b, side, piece])
+
+    def wire_start(b, side):
+        for piece in (0, 1):
+            wire_copy(b, side, piece).start()
 
     weights = [
         pltpu.make_async_copy(src, dst, weight_sem.at[i])
@@ -252,21 +259,21 @@
             src.at[b * rows : (b + 1) * rows], out_hbm[i].at[to : to + rows], out_sem.at[i, b]
         )
 
-    wire_copy(0, 0).start()
+    wire_start(0, 0)
     weights[0].start()
-    wire_copy(0, 1).start()
+    wire_start(0, 1)
     weights[1].start()
     for b in range(1, blocks):
-        wire_copy(b, 0).start()
-        wire_copy(b, 1).start()
+        wire_start(b, 0)
+        wire_start(b, 1)
     if last:
         old_gate.start()
     swap_ref[...] = swap_matrix()
 
-    def widen(b, side, out):
+    def widen(b, side, piece, out):
         def step(p, carry):
             at = pl.multiple_of(side * half + p * sub, sub)
-            for s in range(0, block, 2 * sub):
+            for s in range(piece * near, (piece + 1) * near, 2 * sub):
                 tiles = jnp.concatenate(
                     [
                         wire[b * block + s + d : b * block + s + d + sub, pl.ds(at, sub), :].reshape(
@@ -289,15 +296,17 @@
 
     for b in range(blocks):
         low, high = b * rows, (b + 1) * rows
-        wire_copy(b, 0).wait()
-        widen(b, 0, x_ref)
+        for piece in (0, 1):
+            wire_copy(b, 0, piece).wait()
+            widen(b, 0, piece, x_ref)
         out_copy(0, b).start()
         gates_in = [
             jnp.dot(x_ref[low:high], wg[:, n : n + part], preferred_element_type=f32)
             for n in range(0, hidden, part)
         ]
-        wire_copy(b, 1).wait()
-        widen(b, 1, dy_ref)
+        for piece in (0, 1):
+            wire_copy(b, 1, piece).wait()
+            widen(b, 1, piece, dy_ref)
         out_copy(1, b).start()
         if b == 0:
             for copy in weights:
@@ -426,7 +435,7 @@
             pltpu.VMEM((mine, hidden), bf16),
             pltpu.VMEM((block * count, width), bf16),
             pltpu.VMEM((sub * sub, sub * sub), bf16),
-            pltpu.SemaphoreType.DMA((sources // block, 2)),
+            pltpu.SemaphoreType.DMA((sources // block, 2, 2)),
             pltpu.SemaphoreType.DMA((2,)),
             pltpu.SemaphoreType.DMA((5, sources // block)),
         ]

time: 226 us -> 226 us (level)
  transfers between devices with their start and end apart: 3 -> 3, of which waited for: 3 -> 3; matrix products, arithmetic and copies ran while one was open for 9% -> 9% of each run, Pallas kernels for 12% -> 13%
where the time goes in v5:
time: 226 us
  waiting for transfers between devices  130 us (58%)
  Pallas kernels  49.6 us (22%)
  starting transfers between devices  25.8 us (11%)
  matrix products  19.7 us (9%)
    all_to_all x3, waiting for transfers between devices, exchange(): lax.all_to_all(rows, ('dp', 'expert'), split_axis=0, concat_axis=0, tiled...  130 us
    pallas_call x2, Pallas kernels, expert_rows(): pl.pallas_call(functools.partial(expert_kernel, start, count, block, last...  34.2 us
    all_to_all x3, starting transfers between devices, exchange(): lax.all_to_all(rows, ('dp', 'expert'), split_axis=0, concat_axis=0, tiled...  25.8 us
    pallas_call x2, Pallas kernels, pack(): pl.pallas_call(body, in_specs=in_specs, out_specs=out_specs, out_shape=ou...  10.1 us
    dot_general x1, matrix products, local(): lax.dot_general(rows_x, da, contract_rows, preferred_element_type=f32)  8.27 us
    dot_general x1, matrix products, local(): lax.dot_general(rows_x, db, contract_rows, preferred_element_type=f32)  5.74 us
    dot_general x1, matrix products, local(): lax.dot_general(h, rows_dy, contract_rows, preferred_element_type=f32)  5.64 us
    pallas_call x1, Pallas kernels, combine(): pl.pallas_call(combine_kernel, grid=(1,), in_specs=[pl.BlockSpec(memory_s...  5.42 us
  transfers between devices with their start and end apart: 3, of which 3 were waited for; matrix products, arithmetic and copies ran while one was open for 9% of the time, Pallas kernels for 13%

profile of v5, /device:TPU:1, one launch (start us, length us, event | category | flops | bytes accessed | tf_op | source)
XLA Modules:
  0.0 225.5 jit_solution(1436189325042483300)
XLA Ops:
  0.6 6.4 %pack_first.1 = (bf16[128,224,128]{2,1,0:T(8,128)(2,1)}, s32[16,128]{1,0:T(8,128)}, f32[16,128]{1,0:T(8,128)}, s32[8,128]{1,0:T(8,128)}, s32[8,128]{1,0:T(8,128)}) custom-call(s32[8,128]{1,0:T(8,128)} %bitcast.30, s32[8,128]{1,0:T(8,128)} %bitcast.28, bf16[128,2048]{1,0:T(8,128)(2,1)} %tok_ref.1, bf16[128,2048]{1,0:T(8,128)(2,1)} %dy_ref.1), custom_call_target="tpu_custom_call" | custom-call | bytes 7340032 | tf_op jit(solution)/shard_map/pack_first/pallas_call | solution.py:200
  7.0 11.9 %all-to-all-start.1 = ((bf16[128,224,128]{2,1,0:T(8,128)(2,1)}), bf16[128,224,128]{2,1,0:T(8,128)(2,1)}, u32[]{:S(2)}, u32[]{:S(2)}) async-start(bf16[128,224,128]{2,1,0:T(8,128)(2,1)} %get-tuple-element.29), calls=%async_computation.1 | async-start | bytes 14680064 | tf_op jit(solution)/shard_map/all_to_all | solution.py:528
  18.9 0.0 copy-start
  18.9 3.7 %pack_rest.1 = bf16[128,64,128]{2,1,0:T(8,128)(2,1)} custom-call(s32[16,128]{1,0:T(8,128)} %get-tuple-element.27.index_ref, f32[16,128]{1,0:T(8,128)} %get-tuple-element.28.scale_ref, bf16[128,2048]{1,0:T(8,128)(2,1)} %tok_ref.1, bf16[128,2048]{1,0:T(8,128)(2,1)} %dy_ref.1), custom_call_target="tpu_custom_call" | custom-call | bytes 2097152 | tf_op jit(solution)/shard_map/pack_rest/pallas_call | solution.py:200
  22.6 83.0 %all-to-all-done.1.refs_0_ = bf16[128,224,128]{2,1,0:T(8,128)(2,1)} async-done(((bf16[128,224,128]{2,1,0:T(8,128)(2,1)}), bf16[128,224,128]{2,1,0:T(8,128)(2,1)}, u32[]{:S(2)}, u32[]{:S(2)}) %all-to-all-start.1) | async-done | bytes 7340064 | tf_op jit(solution)/shard_map/all_to_all | solution.py:528
  105.6 8.3 %all-to-all-start = ((bf16[128,64,128]{2,1,0:T(8,128)(2,1)}), bf16[128,64,128]{2,1,0:T(8,128)(2,1)}, u32[]{:S(2)}, u32[]{:S(2)}) async-start(bf16[128,64,128]{2,1,0:T(8,128)(2,1)} %pack_rest.1), calls=%async_computation | async-start | bytes 4194304 | tf_op jit(solution)/shard_map/all_to_all | solution.py:528
  114.0 0.0 copy-done
  114.0 24.8 %expert_rows_first.1 = (bf16[1152,2048]{1,0:T(8,128)(2,1)}, bf16[1152,2048]{1,0:T(8,128)(2,1)}, bf16[1152,768]{1,0:T(8,128)(2,1)}, bf16[1152,768]{1,0:T(8,128)(2...) custom-call(bf16[128,224,128]{2,1,0:T(8,128)(2,1)} %all-to-all-done.1.refs_0_, ...), custom_call_target="tpu_custom_call" | custom-call | flops 14092861440 | bytes 31457280 | tf_op jit(solution)/shard_map/expert_rows_first/pallas_call | solution.py:421
  138.7 5.2 %all-to-all-done.refs_0_ = bf16[128,64,128]{2,1,0:T(8,128)(2,1)} async-done(((bf16[128,64,128]{2,1,0:T(8,128)(2,1)}), bf16[128,64,128]{2,1,0:T(8,128)(2,1)}, u32[]{:S(2)}, u32[]{:S(2)}) %all-to-all-start) | async-done | bytes 2097184 | tf_op jit(solution)/shard_map/all_to_all | solution.py:528
  144.0 9.4 %expert_rows_last.1 = (bf16[1152,2048]{1,0:T(8,128)(2,1)}, bf16[1152,2048]{1,0:T(8,128)(2,1)}, bf16[1152,768]{1,0:T(8,128)(2,1)}, bf16[1152,768]{1,0:T(8,128)(2,...) custom-call(bf16[128,64,128]{2,1,0:T(8,128)(2,1)} %all-to-all-done.r, ...), custom_call_target="tpu_custom_call", output_to_operand_aliasing={{0}: (5, {}), {1}: (6, {}), {2}: (7, {}), {3}: (8, {}), {4}... | custom-call | flops 4026531840 | bytes 15728640 | tf_op jit(solution)/shard_map/expert_rows_last/pallas_call | solution.py:421
  153.4 0.0 copy-start.2
  153.4 0.0 slice-start
  153.4 5.6 %all-to-all-start.2 = ((bf16[128,152,128]{2,1,0:T(8,128)(2,1)}), bf16[128,152,128]{2,1,0:T(8,128)(2,1)}, u32[]{:S(2)}, u32[]{:S(2)}) async-start(bf16[128,152,128]{2,1,0:T(8,128)(2,1)} %get-tuple-element.37), calls=%async_computation.2 | async-start | bytes 9961472 | tf_op jit(solution)/shard_map/all_to_all | solution.py:528
  159.0 0.0 copy-done.2
  159.0 0.0 slice-start.1
  159.0 0.0 copy-start.3
  159.0 0.0 slice-start.2
  159.0 8.3 %fusion = bf16[1,2048,768]{2,1,0:T(8,128)(2,1)} fusion(bf16[1152,2048]{1,0:T(8,128)(2,1)} %get-tuple-element.40, bf16[1152,768]{1,0:T(8,128)(2,1)S(1)} %copy-done.2), kind=kOutput, calls=%fused_computation.3 | convolution fusion | flops 3625451520 | bytes 9633792 | tf_op jit(solution)/shard_map/dot_general | solution.py:543
  167.3 0.0 slice-done
  167.3 0.0 slice-done.1
  167.3 0.0 copy-done.3
  167.3 0.0 slice-start.3
  167.3 0.0 copy-start.1
  167.3 5.7 %fusion.1 = bf16[1,2048,768]{2,1,0:T(8,128)(2,1)} fusion(bf16[1152,2048]{1,0:T(8,128)(2,1)S(1)} %bitcast.21, bf16[1152,768]{1,0:T(8,128)(2,1)S(1)} %copy-done.3), kind=kOutput, calls=%fused_computation.4 | convolution fusion | flops 3625451520 | bytes 9633792 | tf_op jit(solution)/shard_map/dot_general | solution.py:544
  173.1 0.0 slice-done.2
  173.1 0.0 slice-done.3
  173.1 0.0 copy-done.1
  173.1 5.6 %fusion.2 = bf16[1,768,2048]{2,1,0:T(8,128)(2,1)} fusion(bf16[1152,768]{1,0:T(8,128)(2,1)S(1)} %copy-done.1, bf16[1152,2048]{1,0:T(8,128)(2,1)S(1)} %bitcast.23), kind=kOutput, calls=%fused_computation.5 | convolution fusion | flops 3625451520 | bytes 9633792 | tf_op jit(solution)/shard_map/dot_general | solution.py:545
  178.7 41.4 %all-to-all-done.2.back_ref.side_ref = bf16[128,152,128]{2,1,0:T(8,128)(2,1)} async-done(((bf16[128,152,128]{2,1,0:T(8,128)(2,1)}), bf16[128,152,128]{2,1,0:T(8,128)(2,1)}, u32[]{:S(2)}, u32[]{:S(2)}) %all-to-all-start.2) | async-done | bytes 4980768 | tf_op jit(solution)/shard_map/all_to_all | solution.py:528
  220.1 5.4 %combine_rows.1 = (bf16[128,2048]{1,0:T(8,128)(2,1)}, bf16[8,128]{1,0:T(8,128)(2,1)}) custom-call(s32[8,128]{1,0:T(8,128)} %get-tuple-element.25.spot_ref, s32[8,128]{1,0:T(8,128)} %get-tuple-element.26.code_ref, s32[8,128]{1,0:T(8,128)} %bitcast.29, bf16[128,152,128]{2,1,0:T(8,128)(2,1)} %all-to-all-done.2.back_ref.side_ref, ...), custom_call_target="tpu_custom_call" | custom-call | tf_op jit(solution)/shard_map/combine_rows/pallas_call | solution.py:506
  (2 shorter events, 0.0 us)
Async XLA Ops:
  7.0 98.6 %all-to-all-start.1 = ((bf16[128,224,128]{2,1,0:T(8,128)(2,1)}), bf16[128,224,128]{2,1,0:T(8,128)(2,1)}, u32[]{:S(2)}, u32[]{:S(2)}) async-start(bf16[128,224,128]{2,1,0:T(8,128)(2,1)} %get-tuple-element.29), calls=%async_computation.1 | async-start | bytes 14680064 | tf_op jit(solution)/shard_map/all_to_all | solution.py:528
  18.9 95.0 %copy-start = (bf16[1,2048,768]{2,1,0:T(8,128)(2,1)S(1)}, bf16[1,2048,768]{2,1,0:T(8,128)(2,1)}, u32[]{:S(2)}) copy-start(bf16[1,2048,768]{2,1,0:T(8,128)(2,1)} %param.11) | copy-start | bytes 9437188
  105.6 38.3 %all-to-all-start = ((bf16[128,64,128]{2,1,0:T(8,128)(2,1)}), bf16[128,64,128]{2,1,0:T(8,128)(2,1)}, u32[]{:S(2)}, u32[]{:S(2)}) async-start(bf16[128,64,128]{2,1,0:T(8,128)(2,1)} %pack_rest.1), calls=%async_computation | async-start | bytes 4194304 | tf_op jit(solution)/shard_map/all_to_all | solution.py:528
  153.4 5.6 %copy-start.2 = (bf16[1152,768]{1,0:T(8,128)(2,1)S(1)}, bf16[1152,768]{1,0:T(8,128)(2,1)}, u32[]{:S(2)}) copy-start(bf16[1152,768]{1,0:T(8,128)(2,1)} %get-tuple-element.41) | copy-start | bytes 5308420
  153.4 13.9 %slice-start = ((s8[4718592]{0:T(1024)(128)(4,1)}), s8[524288]{0:T(1024)(128)(4,1)S(1)}, s32[]{:S(2)}) async-start(s8[4718592]{0:T(1024)(128)(4,1)} %bitcast.20), calls=%async_computation.3 | async-start | bytes 1048576
  153.4 66.7 %all-to-all-start.2 = ((bf16[128,152,128]{2,1,0:T(8,128)(2,1)}), bf16[128,152,128]{2,1,0:T(8,128)(2,1)}, u32[]{:S(2)}, u32[]{:S(2)}) async-start(bf16[128,152,128]{2,1,0:T(8,128)(2,1)} %get-tuple-element.37), calls=%async_computation.2 | async-start | bytes 9961472 | tf_op jit(solution)/shard_map/all_to_all | solution.py:528
  159.0 8.3 %slice-start.1 = ((s8[4718592]{0:T(1024)(128)(4,1)}), s8[4194304]{0:T(1024)(128)(4,1)S(1)}, s32[]{:S(2)}) async-start(s8[4718592]{0:T(1024)(128)(4,1)} %bitcast.20), calls=%async_computation.4 | async-start | bytes 8388608
  159.0 8.3 %copy-start.3 = (bf16[1152,768]{1,0:T(8,128)(2,1)S(1)}, bf16[1152,768]{1,0:T(8,128)(2,1)}, u32[]{:S(2)}) copy-start(bf16[1152,768]{1,0:T(8,128)(2,1)} %get-tuple-element.42) | copy-start | bytes 5308420
  159.0 14.1 %slice-start.2 = ((s8[4718592]{0:T(1024)(128)(4,1)}), s8[4194304]{0:T(1024)(128)(4,1)S(1)}, s32[]{:S(2)}) async-start(s8[4718592]{0:T(1024)(128)(4,1)} %bitcast.22), calls=%async_computation.5 | async-start | bytes 8388608
  167.3 5.8 %slice-start.3 = ((s8[4718592]{0:T(1024)(128)(4,1)}), s8[524288]{0:T(1024)(128)(4,1)S(1)}, s32[]{:S(2)}) async-start(s8[4718592]{0:T(1024)(128)(4,1)} %bitcast.22), calls=%async_computation.6 | async-start | bytes 1048576
  167.3 5.8 %copy-start.1 = (bf16[1152,768]{1,0:T(8,128)(2,1)S(1)}, bf16[1152,768]{1,0:T(8,128)(2,1)}, u32[]{:S(2)}) copy-start(bf16[1152,768]{1,0:T(8,128)(2,1)} %get-tuple-element.43) | copy-start | bytes 5308420

commit v6 on v5

--- a/solution.py
+++ b/solution.py
@@ -236,7 +236,8 @@
     part = 256
     half = count * sub
 
-    near = block // 2
+    near = 2 * sub
+    pieces = range(block // near)
 
     def wire_copy(b, side, piece):
         low = b * block + piece * near
@@ -244,7 +245,7 @@
         return pltpu.make_async_copy(wire_hbm.at[at], wire.at[at], wire_sem.at[b, side, piece])
 
     def wire_start(b, side):
-        for piece in (0, 1):
+        for piece in pieces:
             wire_copy(b, side, piece).start()
 
     weights = [
@@ -296,7 +297,7 @@
 
     for b in range(blocks):
         low, high = b * rows, (b + 1) * rows
-        for piece in (0, 1):
+        for piece in pieces:
             wire_copy(b, 0, piece).wait()
             widen(b, 0, piece, x_ref)
         out_copy(0, b).start()
@@ -304,7 +305,7 @@
             jnp.dot(x_ref[low:high], wg[:, n : n + part], preferred_element_type=f32)
             for n in range(0, hidden, part)
         ]
-        for piece in (0, 1):
+        for piece in pieces:
             wire_copy(b, 1, piece).wait()
             widen(b, 1, piece, dy_ref)
         out_copy(1, b).start()
@@ -435,7 +436,7 @@
             pltpu.VMEM((mine, hidden), bf16),
             pltpu.VMEM((block * count, width), bf16),
             pltpu.VMEM((sub * sub, sub * sub), bf16),
-            pltpu.SemaphoreType.DMA((sources // block, 2, 2)),
+            pltpu.SemaphoreType.DMA((sources // block, 2, block // (2 * sub))),
             pltpu.SemaphoreType.DMA((2,)),
             pltpu.SemaphoreType.DMA((5, sources // block)),
         ]

time: 226 us -> 226 us (level)
  no operation moved by 1% of the time
where the time goes in v6:
time: 226 us
  waiting for transfers between devices  130 us (58%)
  Pallas kernels  49.9 us (22%)
  starting transfers between devices  25.8 us (11%)
  matrix products  19.7 us (9%)
    all_to_all x3, waiting for transfers between devices, exchange(): lax.all_to_all(rows, ('dp', 'expert'), split_axis=0, concat_axis=0, tiled...  130 us
    pallas_call x2, Pallas kernels, expert_rows(): pl.pallas_call(functools.partial(expert_kernel, start, count, block, last...  34.5 us
    all_to_all x3, starting transfers between devices, exchange(): lax.all_to_all(rows, ('dp', 'expert'), split_axis=0, concat_axis=0, tiled...  25.8 us
    pallas_call x2, Pallas kernels, pack(): pl.pallas_call(body, in_specs=in_specs, out_specs=out_specs, out_shape=ou...  10.1 us
    dot_general x1, matrix products, local(): lax.dot_general(rows_x, da, contract_rows, preferred_element_type=f32)  8.27 us
    dot_general x1, matrix products, local(): lax.dot_general(rows_x, db, contract_rows, preferred_element_type=f32)  5.74 us
    dot_general x1, matrix products, local(): lax.dot_general(h, rows_dy, contract_rows, preferred_element_type=f32)  5.64 us
    pallas_call x1, Pallas kernels, combine(): pl.pallas_call(combine_kernel, grid=(1,), in_specs=[pl.BlockSpec(memory_s...  5.42 us
  transfers between devices with their start and end apart: 3, of which 3 were waited for; matrix products, arithmetic and copies ran while one was open for 9% of the time, Pallas kernels for 13%

profile of v6, /device:TPU:1, one launch (start us, length us, event | category | flops | bytes accessed | tf_op | source)
XLA Modules:
  0.0 225.9 jit_solution(6392678435469445741)
XLA Ops:
  0.6 6.4 %pack_first.1 = (bf16[128,224,128]{2,1,0:T(8,128)(2,1)}, s32[16,128]{1,0:T(8,128)}, f32[16,128]{1,0:T(8,128)}, s32[8,128]{1,0:T(8,128)}, s32[8,128]{1,0:T(8,128)}) custom-call(s32[8,128]{1,0:T(8,128)} %bitcast.30, s32[8,128]{1,0:T(8,128)} %bitcast.28, bf16[128,2048]{1,0:T(8,128)(2,1)} %tok_ref.1, bf16[128,2048]{1,0:T(8,128)(2,1)} %dy_ref.1), custom_call_target="tpu_custom_call" | custom-call | bytes 7340032 | tf_op jit(solution)/shard_map/pack_first/pallas_call | solution.py:200
  7.0 11.9 %all-to-all-start.1 = ((bf16[128,224,128]{2,1,0:T(8,128)(2,1)}), bf16[128,224,128]{2,1,0:T(8,128)(2,1)}, u32[]{:S(2)}, u32[]{:S(2)}) async-start(bf16[128,224,128]{2,1,0:T(8,128)(2,1)} %get-tuple-element.29), calls=%async_computation.1 | async-start | bytes 14680064 | tf_op jit(solution)/shard_map/all_to_all | solution.py:529
  18.9 0.0 copy-start
  18.9 3.7 %pack_rest.1 = bf16[128,64,128]{2,1,0:T(8,128)(2,1)} custom-call(s32[16,128]{1,0:T(8,128)} %get-tuple-element.27.index_ref, f32[16,128]{1,0:T(8,128)} %get-tuple-element.28.scale_ref, bf16[128,2048]{1,0:T(8,128)(2,1)} %tok_ref.1, bf16[128,2048]{1,0:T(8,128)(2,1)} %dy_ref.1), custom_call_target="tpu_custom_call" | custom-call | bytes 2097152 | tf_op jit(solution)/shard_map/pack_rest/pallas_call | solution.py:200
  22.6 83.0 %all-to-all-done.1.refs_0_ = bf16[128,224,128]{2,1,0:T(8,128)(2,1)} async-done(((bf16[128,224,128]{2,1,0:T(8,128)(2,1)}), bf16[128,224,128]{2,1,0:T(8,128)(2,1)}, u32[]{:S(2)}, u32[]{:S(2)}) %all-to-all-start.1) | async-done | bytes 7340064 | tf_op jit(solution)/shard_map/all_to_all | solution.py:529
  105.6 8.3 %all-to-all-start = ((bf16[128,64,128]{2,1,0:T(8,128)(2,1)}), bf16[128,64,128]{2,1,0:T(8,128)(2,1)}, u32[]{:S(2)}, u32[]{:S(2)}) async-start(bf16[128,64,128]{2,1,0:T(8,128)(2,1)} %pack_rest.1), calls=%async_computation | async-start | bytes 4194304 | tf_op jit(solution)/shard_map/all_to_all | solution.py:529
  114.0 0.0 copy-done
  114.0 24.8 %expert_rows_first.1 = (bf16[1152,2048]{1,0:T(8,128)(2,1)}, bf16[1152,2048]{1,0:T(8,128)(2,1)}, bf16[1152,768]{1,0:T(8,128)(2,1)}, bf16[1152,768]{1,0:T(8,128)(2...) custom-call(bf16[128,224,128]{2,1,0:T(8,128)(2,1)} %all-to-all-done.1.refs_0_, ...), custom_call_target="tpu_custom_call" | custom-call | flops 14092861440 | bytes 31457280 | tf_op jit(solution)/shard_map/expert_rows_first/pallas_call | solution.py:422
  138.7 5.2 %all-to-all-done.refs_0_ = bf16[128,64,128]{2,1,0:T(8,128)(2,1)} async-done(((bf16[128,64,128]{2,1,0:T(8,128)(2,1)}), bf16[128,64,128]{2,1,0:T(8,128)(2,1)}, u32[]{:S(2)}, u32[]{:S(2)}) %all-to-all-start) | async-done | bytes 2097184 | tf_op jit(solution)/shard_map/all_to_all | solution.py:529
  144.0 9.7 %expert_rows_last.1 = (bf16[1152,2048]{1,0:T(8,128)(2,1)}, bf16[1152,2048]{1,0:T(8,128)(2,1)}, bf16[1152,768]{1,0:T(8,128)(2,1)}, bf16[1152,768]{1,0:T(8,128)(2,...) custom-call(bf16[128,64,128]{2,1,0:T(8,128)(2,1)} %all-to-all-done.r, ...), custom_call_target="tpu_custom_call", output_to_operand_aliasing={{0}: (5, {}), {1}: (6, {}), {2}: (7, {}), {3}: (8, {}), {4}... | custom-call | flops 4026531840 | bytes 15728640 | tf_op jit(solution)/shard_map/expert_rows_last/pallas_call | solution.py:422
  153.7 0.0 copy-start.2
  153.7 0.0 slice-start
  153.7 5.6 %all-to-all-start.2 = ((bf16[128,152,128]{2,1,0:T(8,128)(2,1)}), bf16[128,152,128]{2,1,0:T(8,128)(2,1)}, u32[]{:S(2)}, u32[]{:S(2)}) async-start(bf16[128,152,128]{2,1,0:T(8,128)(2,1)} %get-tuple-element.37), calls=%async_computation.2 | async-start | bytes 9961472 | tf_op jit(solution)/shard_map/all_to_all | solution.py:529
  159.3 0.0 copy-done.2
  159.3 0.0 slice-start.1
  159.3 0.0 copy-start.3
  159.3 0.0 slice-start.2
  159.4 8.3 %fusion = bf16[1,2048,768]{2,1,0:T(8,128)(2,1)} fusion(bf16[1152,2048]{1,0:T(8,128)(2,1)} %get-tuple-element.40, bf16[1152,768]{1,0:T(8,128)(2,1)S(1)} %copy-done.2), kind=kOutput, calls=%fused_computation.3 | convolution fusion | flops 3625451520 | bytes 9633792 | tf_op jit(solution)/shard_map/dot_general | solution.py:544
  167.6 0.0 slice-done
  167.6 0.0 slice-done.1
  167.6 0.0 copy-done.3
  167.6 0.0 slice-start.3
  167.7 0.0 copy-start.1
  167.7 5.7 %fusion.1 = bf16[1,2048,768]{2,1,0:T(8,128)(2,1)} fusion(bf16[1152,2048]{1,0:T(8,128)(2,1)S(1)} %bitcast.21, bf16[1152,768]{1,0:T(8,128)(2,1)S(1)} %copy-done.3), kind=kOutput, calls=%fused_computation.4 | convolution fusion | flops 3625451520 | bytes 9633792 | tf_op jit(solution)/shard_map/dot_general | solution.py:545
  173.4 0.0 slice-done.2
  173.4 0.0 slice-done.3
  173.4 0.0 copy-done.1
  173.4 5.6 %fusion.2 = bf16[1,768,2048]{2,1,0:T(8,128)(2,1)} fusion(bf16[1152,768]{1,0:T(8,128)(2,1)S(1)} %copy-done.1, bf16[1152,2048]{1,0:T(8,128)(2,1)S(1)} %bitcast.23), kind=kOutput, calls=%fused_computation.5 | convolution fusion | flops 3625451520 | bytes 9633792 | tf_op jit(solution)/shard_map/dot_general | solution.py:546
  179.1 41.4 %all-to-all-done.2.back_ref.side_ref = bf16[128,152,128]{2,1,0:T(8,128)(2,1)} async-done(((bf16[128,152,128]{2,1,0:T(8,128)(2,1)}), bf16[128,152,128]{2,1,0:T(8,128)(2,1)}, u32[]{:S(2)}, u32[]{:S(2)}) %all-to-all-start.2) | async-done | bytes 4980768 | tf_op jit(solution)/shard_map/all_to_all | solution.py:529
  220.4 5.4 %combine_rows.1 = (bf16[128,2048]{1,0:T(8,128)(2,1)}, bf16[8,128]{1,0:T(8,128)(2,1)}) custom-call(s32[8,128]{1,0:T(8,128)} %get-tuple-element.25.spot_ref, s32[8,128]{1,0:T(8,128)} %get-tuple-element.26.code_ref, s32[8,128]{1,0:T(8,128)} %bitcast.29, bf16[128,152,128]{2,1,0:T(8,128)(2,1)} %all-to-all-done.2.back_ref.side_ref, ...), custom_call_target="tpu_custom_call" | custom-call | tf_op jit(solution)/shard_map/combine_rows/pallas_call | solution.py:507
  (2 shorter events, 0.0 us)
Async XLA Ops:
  7.0 98.6 %all-to-all-start.1 = ((bf16[128,224,128]{2,1,0:T(8,128)(2,1)}), bf16[128,224,128]{2,1,0:T(8,128)(2,1)}, u32[]{:S(2)}, u32[]{:S(2)}) async-start(bf16[128,224,128]{2,1,0:T(8,128)(2,1)} %get-tuple-element.29), calls=%async_computation.1 | async-start | bytes 14680064 | tf_op jit(solution)/shard_map/all_to_all | solution.py:529
  18.9 95.0 %copy-start = (bf16[1,2048,768]{2,1,0:T(8,128)(2,1)S(1)}, bf16[1,2048,768]{2,1,0:T(8,128)(2,1)}, u32[]{:S(2)}) copy-start(bf16[1,2048,768]{2,1,0:T(8,128)(2,1)} %param.11) | copy-start | bytes 9437188
  105.6 38.3 %all-to-all-start = ((bf16[128,64,128]{2,1,0:T(8,128)(2,1)}), bf16[128,64,128]{2,1,0:T(8,128)(2,1)}, u32[]{:S(2)}, u32[]{:S(2)}) async-start(bf16[128,64,128]{2,1,0:T(8,128)(2,1)} %pack_rest.1), calls=%async_computation | async-start | bytes 4194304 | tf_op jit(solution)/shard_map/all_to_all | solution.py:529
  153.7 5.6 %copy-start.2 = (bf16[1152,768]{1,0:T(8,128)(2,1)S(1)}, bf16[1152,768]{1,0:T(8,128)(2,1)}, u32[]{:S(2)}) copy-start(bf16[1152,768]{1,0:T(8,128)(2,1)} %get-tuple-element.41) | copy-start | bytes 5308420
  153.7 13.9 %slice-start = ((s8[4718592]{0:T(1024)(128)(4,1)}), s8[524288]{0:T(1024)(128)(4,1)S(1)}, s32[]{:S(2)}) async-start(s8[4718592]{0:T(1024)(128)(4,1)} %bitcast.20), calls=%async_computation.3 | async-start | bytes 1048576
  153.7 66.7 %all-to-all-start.2 = ((bf16[128,152,128]{2,1,0:T(8,128)(2,1)}), bf16[128,152,128]{2,1,0:T(8,128)(2,1)}, u32[]{:S(2)}, u32[]{:S(2)}) async-start(bf16[128,152,128]{2,1,0:T(8,128)(2,1)} %get-tuple-element.37), calls=%async_computation.2 | async-start | bytes 9961472 | tf_op jit(solution)/shard_map/all_to_all | solution.py:529
  159.3 8.3 %slice-start.1 = ((s8[4718592]{0:T(1024)(128)(4,1)}), s8[4194304]{0:T(1024)(128)(4,1)S(1)}, s32[]{:S(2)}) async-start(s8[4718592]{0:T(1024)(128)(4,1)} %bitcast.20), calls=%async_computation.4 | async-start | bytes 8388608
  159.3 8.3 %copy-start.3 = (bf16[1152,768]{1,0:T(8,128)(2,1)S(1)}, bf16[1152,768]{1,0:T(8,128)(2,1)}, u32[]{:S(2)}) copy-start(bf16[1152,768]{1,0:T(8,128)(2,1)} %get-tuple-element.42) | copy-start | bytes 5308420
  159.3 14.1 %slice-start.2 = ((s8[4718592]{0:T(1024)(128)(4,1)}), s8[4194304]{0:T(1024)(128)(4,1)S(1)}, s32[]{:S(2)}) async-start(s8[4718592]{0:T(1024)(128)(4,1)} %bitcast.22), calls=%async_computation.5 | async-start | bytes 8388608
  167.6 5.8 %slice-start.3 = ((s8[4718592]{0:T(1024)(128)(4,1)}), s8[524288]{0:T(1024)(128)(4,1)S(1)}, s32[]{:S(2)}) async-start(s8[4718592]{0:T(1024)(128)(4,1)} %bitcast.22), calls=%async_computation.6 | async-start | bytes 1048576
  167.7 5.8 %copy-start.1 = (bf16[1152,768]{1,0:T(8,128)(2,1)S(1)}, bf16[1152,768]{1,0:T(8,128)(2,1)}, u32[]{:S(2)}) copy-start(bf16[1152,768]{1,0:T(8,128)(2,1)} %get-tuple-element.43) | copy-start | bytes 5308420
